TPU v7x, 256 devices: a whole 4x4x8 slice. The times are simulated.
256 devices in a mesh: tiles: 64 (over x, z, core), diag: 4 (over y).
Axes of the slice: x: 4, y: 4, z: 8, core: 2. Of those that a mesh axis runs over, the one named last changes fastest.
Arguments:
- inputs: bfloat16 [48, 8192, 512], P(None, 'tiles', 'diag'), may hold values from -6 to 6
- cotangent: bfloat16 [48, 8192, 512], P(None, 'tiles', 'diag'), may hold values from -6 to 6
- conv_weight: bfloat16 [9, 48, 48], replicated, may hold values from -0.3125 to 0.3125
- mix_weight: bfloat16 [48, 48], replicated, may hold values from -0.875 to 0.875
- counts: int32 [64], P('tiles'), may hold values from 1 to 4, 128 in all
- band_reach: int32 [256], P('tiles'), may hold values from 256 to 512
- dilation: int32 [2], replicated, may hold values from 1 to 8, as said below
Outputs:
- grad_inputs: bfloat16 [48, 8192, 512], P(None, 'tiles', 'diag')
- grad_conv: float32 [9, 48, 48], replicated
- grad_mix: float32 [48, 48], replicated
Inputs may be any that keep to these rules, and one draw needn't show every extreme that they name: `counts`: the live tiles of the tiles indices, taken in order, are the consecutive tiles of the band; some index holds 4. `band_reach`: offsets at or beyond a slot's reach are empty cells; entries of empty slots are ignored. `dilation`: one of the two dilations equals 8, the other is smaller.
All inputs are finite; a program needn't handle non-finite values. No bound on the sum of `counts` on one device may be relied on, other than what follows from the above.
Results may differ from a plain program's by a relative error of at most 0.009.
Values may be sent and summed in bfloat16 or wider, within the bound.
A program may use at most 192 MiB of HBM per device.

v0:
```python
import math

import jax
import jax.numpy as jnp
from jax import lax
from jax.sharding import PartitionSpec as P

TPD = 2
DMAX = 8


def with_halo(value, sides, width):
    for axis, dim in sides:
        size, length = (lax.axis_size(axis), value.shape[dim])
        up = [(i, (i + 1) % size) for i in range(size - 1)]
        down = [(j, i) for i, j in up]
        last = lax.slice_in_dim(value, length - width, length, axis=dim)
        initial = lax.slice_in_dim(value, 0, width, axis=dim)
        before = lax.ppermute(last, axis, up)
        after = lax.ppermute(initial, axis, down)
        value = jnp.concatenate([before, value, after], axis=dim)
    return value


def stencil_offsets(dilation):
    result = []
    for row_step in range(3):
        for col_step in range(3):
            row_move = (row_step - 1) * dilation[0]
            col_move = (col_step - 1) * dilation[1]
            result.append((row_move, col_move - row_move))
    return result


def window(field, row_start, col_start, row_count, band_cols):
    return lax.dynamic_slice(
        field, (jnp.int32(0), row_start, col_start), (field.shape[0], row_count, band_cols)
    )


def edge_pair(field, live_rows, depth):
    first = field[:, :depth]
    last = lax.dynamic_slice_in_dim(field, live_rows - depth, depth, 1)
    return jnp.concatenate([first, last], axis=1)


def stitch(field, received, live_rows, depth):
    top_rows = received[:, :depth]
    bottom_rows = received[:, 3 * depth :]
    joined = jnp.concatenate([top_rows, field, jnp.zeros_like(top_rows)], axis=1)
    return lax.dynamic_update_slice_in_dim(joined, bottom_rows, live_rows + depth, 1)


def extend(field, live_rows):
    wide = with_halo(field, (("diag", 2),), 2 * DMAX)
    received = with_halo(edge_pair(wide, live_rows, DMAX), (("tiles", 1),), DMAX)
    return stitch(wide, received, live_rows, DMAX)


def mix_channels(weight, field):
    return lax.dot_general(
        weight, field, (((1,), (0,)), ((), ())), preferred_element_type=jnp.float32
    )


def mix_back(weight, field):
    return lax.dot_general(
        weight, field, (((0,), (0,)), ((), ())), preferred_element_type=jnp.float32
    )


def contract(left, right):
    return lax.dot_general(
        left, right, (((1, 2), (1, 2)), ((), ())), preferred_element_type=jnp.float32
    )


def body(inputs, cotangent, conv_weight, mix_weight, counts, band_reach, dilation):
    chans, row_count, band_cols = inputs.shape
    tile_rows = row_count // band_reach.shape[0]
    live_rows = counts[0] * tile_rows
    row_ids = lax.broadcasted_iota(jnp.int32, (row_count, band_cols), 0)
    offset_ids = (
        lax.broadcasted_iota(jnp.int32, (row_count, band_cols), 1)
        + lax.axis_index("diag") * band_cols
    )
    row_reach = jnp.repeat(band_reach, tile_rows)
    live = row_ids < live_rows
    keep = live & (offset_ids < row_reach[:, None])
    rectified = jnp.where(keep[None], jnp.maximum(inputs, 0), 0)
    masked = jnp.where(keep[None], cotangent, 0)
    shifts = stencil_offsets(dilation)
    grown = extend(rectified, live_rows)
    pre_act = jnp.zeros((chans, row_count, band_cols), jnp.float32)
    for stencil in range(9):
        row_move, band_move = shifts[stencil]
        tapped = window(grown, DMAX + row_move, 2 * DMAX + band_move, row_count, band_cols)
        pre_act = pre_act + mix_channels(conv_weight[stencil], tapped)
    back = mix_back(mix_weight, masked)
    grad_pre = jnp.where(pre_act > 0, back, 0).astype(jnp.bfloat16)
    grad_grown = extend(grad_pre, live_rows)
    hidden = jnp.maximum(pre_act, 0).astype(jnp.bfloat16)
    mix_part = contract(masked, hidden)
    conv_terms = []
    for stencil in range(9):
        row_move, band_move = shifts[stencil]
        tapped = window(grown, DMAX + row_move, 2 * DMAX + band_move, row_count, band_cols)
        conv_terms.append(contract(grad_pre, tapped))
    conv_part = jnp.stack(conv_terms)
    spread = jnp.zeros((chans, row_count, band_cols), jnp.float32)
    for stencil in range(9):
        row_move, band_move = shifts[stencil]
        tapped = window(grad_grown, DMAX - row_move, 2 * DMAX - band_move, row_count, band_cols)
        spread = spread + mix_back(conv_weight[stencil], tapped)
    active = keep[None] & (inputs > 0)
    total_grad = cotangent.astype(jnp.float32) + jnp.where(active, spread, 0.0)
    grad_inputs = jnp.where(live[None], total_grad, 0.0).astype(jnp.bfloat16)
    conv_sum, mix_sum = lax.psum((conv_part, mix_part), ("tiles", "diag"))
    cells = TPD * lax.axis_size("tiles") * tile_rows * band_cols * lax.axis_size("diag")
    scale = 1.0 / math.sqrt(cells)
    return (grad_inputs, conv_sum * scale, mix_sum * scale)


def solution(mesh):
    in_specs = (
        P(None, "tiles", "diag"),
        P(None, "tiles", "diag"),
        P(),
        P(),
        P("tiles"),
        P("tiles"),
        P(),
    )
    out_specs = (P(None, "tiles", "diag"), P(), P())
    return jax.shard_map(body, mesh=mesh, in_specs=in_specs, out_specs=out_specs, check_vma=False)
```

profile of v0, /device:TPU:1, one launch (start us, length us, event | category | flops | bytes accessed | tf_op | source)
XLA Modules:
  0.0 461.1 jit_solution(15554202892198312277)
XLA Ops:
  8.8 2.5 maximum_select_fusion
  13.0 1.9 copy.28
  14.9 4.7 %collective-permute-start = (bf16[48,128,16]{1,2,0:T(8,128)(2,1)S(1)}, bf16[48,128,16]{1,2,0:T(8,128)(2,1)}, u32[]{:S(2)}, u32[]{:S(2)}) collective-permute-start(bf16[48,128,16]{1,2,0:T(8,128)(2,1)S(1)} %copy.28), channel_id=1, source_target_pairs={{0,1},{1,2},{2,3},{4,5},{5,6},{6,7},{8,9},{9,10},{10,11},{12,13},{... | collective-permute-start | bytes 589832 | tf_op jit(solution)/shard_map/ppermute | solution.py:19
  24.3 4.5 collective-permute-done.1
  28.8 2.5 copy.31
  31.3 3.2 pad_maximum_fusion
  35.3 5.3 %collective-permute-start.2 = (bf16[48,8,160]{2,0,1:T(8,128)(2,1)}, bf16[48,8,160]{2,0,1:T(8,128)(2,1)}, u32[]{:S(2)}, u32[]{:S(2)}) collective-permute-start(bf16[48,8,160]{2,0,1:T(8,128)(2,1)} %get-tuple-element.12), channel_id=1, source_target_pairs={{0,4},{4,8},{8,12},{12,16},{16,20},{20,24},{24,28},{28,32},{32,36}... | collective-permute-start | bytes 368648 | tf_op jit(solution)/shard_map/ppermute | solution.py:19
  52.5 2.1 collective-permute-start.3
  54.6 5.5 %maximum_maximum_fusion = bf16[48,144,160]{2,0,1:T(8,128)(2,1)S(1)} fusion(bf16[48,128,16]{2,0,1:T(8,128)(2,1)} %copy.31, bf16[48,128,128]{2,0,1:T(8,128)(2,1)S(1)} %maximum_select_fusion, bf16[48,128,16]{2,0,1:T(8,128)(2,1)S(1)} %copy.30, bf16[48,8,160]{2,0,1:T(8,128)(2,1)} %collective-permute-done.2, bf16[144]{0:T(256)(128)(2,1)S(1)} %pad.12.clone), kind=kLoop, calls=%fused_computation | loop fusion | flops 11059200 | bytes 4301088 | tf_op jit(solution)/shard_map/concatenate | solution.py:50
  60.1 2.7 fusion.30
  64.3 2.4 fusion.34
  66.7 2.4 fusion.38
  71.3 6.1 %add_add_fusion = f32[128,128,48]{1,2,0:T(8,128)S(1)} fusion(f32[128,128,48]{1,2,0:T(8,128)S(1)} %fusion.48, f32[128,128,48]{1,2,0:T(8,128)S(1)} %fusion.52, f32[128,128,48]{1,2,0:T(8,128)} %fusion.34, f32[128,128,48]{1,2,0:T(8,128)} %fusion.30, f32[128,128,48]{1,2,0:T(8,128)} %fusion.38, f32[128,128,48]{1,2,0:T(8,128)S(1)} %fusion.56, ...), kind=kOutput, calls=%fused_computation.10 | convolution fusion | flops 81788928 | bytes 29896712 | tf_op jit(solution)/shard_map/dot_general | solution.py:61
  77.5 2.3 fusion.121
  83.9 78.8 %psum.15 = f32[48,48]{1,0:T(8,128)S(1)} all-reduce(f32[48,48]{1,0:T(8,128)} %fusion.121), channel_id=1, replica_groups=mesh['tiles'=64,'diag'=4] {'tiles','diag'}, use_global_device_ids=true, to_apply=%region_1.2 | all-reduce | flops 2304 | bytes 18432 | tf_op jit(solution)/shard_map/psum | solution.py:118
  162.8 2.8 fusion.76
  165.6 2.7 fusion.82
  173.8 2.5 copy.34
  178.5 4.7 %collective-permute-start.4 = (bf16[48,128,16]{1,2,0:T(8,128)(2,1)}, bf16[48,128,16]{1,2,0:T(8,128)(2,1)}, u32[]{:S(2)}, u32[]{:S(2)}) collective-permute-start(bf16[48,128,16]{1,2,0:T(8,128)(2,1)} %copy.34), channel_id=1, source_target_pairs={{0,1},{1,2},{2,3},{4,5},{5,6},{6,7},{8,9},{9,10},{10,11},{12,13},{... | collective-permute-start | bytes 589832 | tf_op jit(solution)/shard_map/ppermute | solution.py:19
  183.8 2.3 collective-permute-done.4
  187.9 2.5 copy.37
  190.4 3.2 pad_maximum_fusion.1
  194.3 4.0 collective-permute-start.6
  198.3 220.1 %all-reduce.2.cloned.1.call-done = f32[9,48,48]{2,1,0:T(8,128)} async-done(((f32[9,48,48]{2,1,0:T(8,128)}), f32[9,48,48]{2,1,0:T(8,128)}) %all-reduce.2.cloned.1.call-update) | async-done | bytes 82960 | tf_op jit(solution)/shard_map/psum | solution.py:118
  420.1 2.9 collective-permute-start.7
  423.0 5.3 %maximum_maximum_fusion.1 = bf16[48,144,160]{2,0,1:T(8,128)(2,1)S(1)} fusion(bf16[48,128,16]{2,0,1:T(8,128)(2,1)} %copy.37, bf16[48,128,128]{2,0,1:T(8,128)(2,1)S(1)} %fusion.6, bf16[48,128,16]{2,0,1:T(8,128)(2,1)S(1)} %copy.36, bf16[48,8,160]{2,0,1:T(8,128)(2,1)} %collective-permute-done.6, bf16[144]{0:T(256)(128)(2,1)S(1)} %pad.12.clone), kind=kLoop, calls=%fused_computation.1 | loop fusion | flops 11059200 | bytes 4301088 | tf_op jit(solution)/shard_map/concatenate | solution.py:50
  428.4 2.4 fusion.7
  432.2 2.4 fusion.18
  434.5 2.4 fusion.20
  438.4 2.4 fusion.26
  440.7 10.3 %fusion.2 = bf16[48,128,128]{2,0,1:T(8,128)(2,1)} fusion(f32[128,128,48]{1,2,0:T(8,128)S(1)} %fusion.14, f32[128,128,48]{1,2,0:T(8,128)S(1)} %fusion.16, f32[128,128,48]{1,2,0:T(8,128)} %fusion.18, f32[128,128,48]{1,2,0:T(8,128)} %fusion.7, f32[128,128,48]{1,2,0:T(8,128)} %fusion.20, f32[128,128,48]{1,2,0:T(8,128)S(1)} %fusion.22, ...), kind=kOutput, calls=%fused_computation.7 | convolution fusion | flops 88866816 | bytes 31486472 | tf_op jit(solution)/shard_map/dot_general | solution.py:67
  451.1 3.0 copy.47
  (67 shorter events, 31.8 us)
Async XLA Ops:
  7.2 72.6 %copy-start = (bf16[48,48]{1,0:T(8,128)(2,1)S(1)}, bf16[48,48]{1,0:T(8,128)(2,1)}, u32[]{:S(2)}) copy-start(bf16[48,48]{1,0:T(8,128)(2,1)} %param.10) | copy-start | bytes 13828
  7.2 411.3 %all-reduce.2.cloned.1.call-start = ((), (), s32[]{:S(2)}) async-start(), calls=%async_computation | async-start | bytes 442368 | tf_op jit(solution)/shard_map/psum | solution.py:118
  14.9 7.6 %collective-permute-start = (bf16[48,128,16]{1,2,0:T(8,128)(2,1)S(1)}, bf16[48,128,16]{1,2,0:T(8,128)(2,1)}, u32[]{:S(2)}, u32[]{:S(2)}) collective-permute-start(bf16[48,128,16]{1,2,0:T(8,128)(2,1)S(1)} %copy.28), channel_id=1, source_target_pairs={{0,1},{1,2},{2,3},{4,5},{5,6},{6,7},{8,9},{9,10},{10,11},{12,13},{... | collective-permute-start | bytes 589832 | tf_op jit(solution)/shard_map/ppermute | solution.py:19
  21.2 7.7 %collective-permute-start.1 = (bf16[48,128,16]{1,2,0:T(8,128)(2,1)}, bf16[48,128,16]{1,2,0:T(8,128)(2,1)}, u32[]{:S(2)}, u32[]{:S(2)}) collective-permute-start(bf16[48,128,16]{1,2,0:T(8,128)(2,1)} %copy.29), channel_id=1, source_target_pairs={{1,0},{2,1},{3,2},{5,4},{6,5},{7,6},{9,8},{10,9},{11,10},{13,12},{... | collective-permute-start | bytes 589832 | tf_op jit(solution)/shard_map/ppermute | solution.py:20
  31.3 9.2 %copy-start.9 = (s32[2]{0:T(128)S(1)}, s32[2]{0:T(128)}, u32[]{:S(2)}) copy-start(s32[2]{0:T(128)} %param.13) | copy-start | bytes 28
  35.3 19.3 %collective-permute-start.2 = (bf16[48,8,160]{2,0,1:T(8,128)(2,1)}, bf16[48,8,160]{2,0,1:T(8,128)(2,1)}, u32[]{:S(2)}, u32[]{:S(2)}) collective-permute-start(bf16[48,8,160]{2,0,1:T(8,128)(2,1)} %get-tuple-element.12), channel_id=1, source_target_pairs={{0,4},{4,8},{8,12},{12,16},{16,20},{20,24},{24,28},{28,32},{32,36}... | collective-permute-start | bytes 368648 | tf_op jit(solution)/shard_map/ppermute | solution.py:19
  52.5 7.6 %copy-start.7 = (bf16[9,48,48]{2,1,0:T(8,128)(2,1)S(1)}, bf16[9,48,48]{2,1,0:T(8,128)(2,1)}, u32[]{:S(2)}) copy-start(bf16[9,48,48]{2,1,0:T(8,128)(2,1)} %param.9) | copy-start | bytes 124420
  52.5 7.6 %collective-permute-start.3 = (bf16[48,8,160]{2,0,1:T(8,128)(2,1)}, bf16[48,8,160]{2,0,1:T(8,128)(2,1)S(1)}, u32[]{:S(2)}, u32[]{:S(2)}) collective-permute-start(bf16[48,8,160]{2,0,1:T(8,128)(2,1)} %get-tuple-element.11), channel_id=1, source_target_pairs={{4,0},{8,4},{12,8},{16,12},{20,16},{24,20},{28,24},{32,28},{36,32}... | collective-permute-start | bytes 368648 | tf_op jit(solution)/shard_map/ppermute | solution.py:20
  60.1 21.3 %copy-start.2 = (bf16[48,144,160]{2,0,1:T(8,128)(2,1)}, bf16[48,144,160]{2,0,1:T(8,128)(2,1)S(1)}, u32[]{:S(2)}) copy-start(bf16[48,144,160]{2,0,1:T(8,128)(2,1)S(1)} %constant_dynamic-update-slice_fusion.1) | copy-start | bytes 6635524
  71.3 6.1 %copy-start.5 = (bf16[48,128,128]{2,1,0:T(8,128)(2,1)S(1)}, bf16[48,128,128]{2,1,0:T(8,128)(2,1)}, u32[]{:S(2)}) copy-start(bf16[48,128,128]{2,1,0:T(8,128)(2,1)} %param.8) | copy-start | bytes 4718596
  77.4 2.3 copy-start.6
  162.8 5.5 %copy-start.3 = (bf16[48,144,160]{2,0,1:T(8,128)(2,1)S(1)}, bf16[48,144,160]{2,0,1:T(8,128)(2,1)}, u32[]{:S(2)}) copy-start(bf16[48,144,160]{2,0,1:T(8,128)(2,1)} %copy-done.2) | copy-start | bytes 6635524
  173.0 0.7 copy-start.8
  177.2 10.7 %collective-permute-start.5 = (bf16[48,128,16]{1,2,0:T(8,128)(2,1)S(1)}, bf16[48,128,16]{1,2,0:T(8,128)(2,1)}, u32[]{:S(2)}, u32[]{:S(2)}) collective-permute-start(bf16[48,128,16]{1,2,0:T(8,128)(2,1)S(1)} %copy.35), channel_id=1, source_target_pairs={{1,0},{2,1},{3,2},{5,4},{6,5},{7,6},{9,8},{10,9},{11,10},{13,12},{... | collective-permute-start | bytes 589832 | tf_op jit(solution)/shard_map/ppermute | solution.py:20
  178.5 7.6 %collective-permute-start.4 = (bf16[48,128,16]{1,2,0:T(8,128)(2,1)}, bf16[48,128,16]{1,2,0:T(8,128)(2,1)}, u32[]{:S(2)}, u32[]{:S(2)}) collective-permute-start(bf16[48,128,16]{1,2,0:T(8,128)(2,1)} %copy.34), channel_id=1, source_target_pairs={{0,1},{1,2},{2,3},{4,5},{5,6},{6,7},{8,9},{9,10},{10,11},{12,13},{... | collective-permute-start | bytes 589832 | tf_op jit(solution)/shard_map/ppermute | solution.py:19
  194.3 228.7 %collective-permute-start.6 = (bf16[48,8,160]{2,0,1:T(8,128)(2,1)}, bf16[48,8,160]{2,0,1:T(8,128)(2,1)}, u32[]{:S(2)}, u32[]{:S(2)}) collective-permute-start(bf16[48,8,160]{2,0,1:T(8,128)(2,1)} %get-tuple-element.10), channel_id=1, source_target_pairs={{0,4},{4,8},{8,12},{12,16},{16,20},{20,24},{24,28},{28,32},{32,36}... | collective-permute-start | bytes 368648 | tf_op jit(solution)/shard_map/ppermute | solution.py:19
  420.1 8.2 %collective-permute-start.7 = (bf16[48,8,160]{2,0,1:T(8,128)(2,1)}, bf16[48,8,160]{2,0,1:T(8,128)(2,1)S(1)}, u32[]{:S(2)}, u32[]{:S(2)}) collective-permute-start(bf16[48,8,160]{2,0,1:T(8,128)(2,1)} %get-tuple-element.9), channel_id=1, source_target_pairs={{4,0},{8,4},{12,8},{16,12},{20,16},{24,20},{28,24},{32,28},{36,32}... | collective-permute-start | bytes 368648 | tf_op jit(solution)/shard_map/ppermute | solution.py:20
  438.4 2.4 copy-start.4
  440.7 13.3 %copy-start.1 = (bf16[48,48]{1,0:T(8,128)(2,1)S(1)}, bf16[48,48]{1,0:T(8,128)(2,1)}, u32[]{:S(2)}) copy-start(bf16[48,48]{1,0:T(8,128)(2,1)} %param.10) | copy-start | bytes 13828
Sparse Core Ops, SparseCore 0:
  173.9 244.5 all-reduce.1
where the time goes:
time: 468 us; the launch traced here: 461 us
  waiting for transfers between devices  227 us (49%)
  blocking collectives  78.8 us (17%)
  matrix products  54.9 us (12%)
  between operations  26.5 us (6%)
  starting transfers between devices  26.2 us (6%)
  local copies, waits for them, and re-layouts  25.6 us (5%)
  other arithmetic  22 us (5%)
    psum x1, waiting for transfers between devices, body(): conv_sum, mix_sum = lax.psum((conv_part, mix_part), ('tiles', 'diag'))  220 us
    psum x1, blocking collectives, body(): conv_sum, mix_sum = lax.psum((conv_part, mix_part), ('tiles', 'diag'))  78.8 us
    dot_general x10, matrix products, mix_back(): lax.dot_general(weight, field, (((0,), (0,)), ((), ())), preferred_elemen...  24.3 us
    ppermute x4, starting transfers between devices, with_halo(): before = lax.ppermute(last, axis, up)  18.7 us
    dot_general x9, matrix products, mix_channels(): lax.dot_general(weight, field, (((1,), (0,)), ((), ())), preferred_elemen...  17.3 us
    dot_general x10, matrix products, contract(): lax.dot_general(left, right, (((1, 2), (1, 2)), ((), ())), preferred_elem...  13.3 us
    concatenate x2, other arithmetic, stitch(): jnp.concatenate([top_rows, field, jnp.zeros_like(top_rows)], axis=1)  10.8 us
  transfers between devices with their start and end apart: 9, of which 3 were waited for; matrix products, arithmetic and copies ran while one was open for 6% of the time, Pallas kernels for 0%

commit v1 on v0

v1 whole, which is shorter than its diff:
```python
import functools
import math

import jax
import jax.numpy as jnp
from jax import lax
from jax.experimental import pallas as pl
from jax.experimental.pallas import tpu as pltpu
from jax.sharding import PartitionSpec as P

MESH = pl.DeviceIdType.MESH
TPD = 2
DMAX = 8
CH = 48
ROWS = 128
COLS = 128
EDGE = 2 * DMAX
GROUPS = COLS // EDGE
STEP = 8
TAPS = 9
SHARES = 16
KPAD = 512
VMEM_LIMIT = 56 * 1024 * 1024
BF = jnp.bfloat16
F32 = jnp.float32
LIVE, REACH, DIL, TILE, DIAG, LAST_TILE, LAST_DIAG = 0, 1, 5, 7, 8, 9, 10


def iota(shape, dim):
    return lax.broadcasted_iota(jnp.int32, shape, dim)


def reach_of(par, ids):
    reach = jnp.where(ids < 64, jnp.where(ids < 32, par[REACH], par[REACH + 1]),
                      jnp.where(ids < 96, par[REACH + 2], par[REACH + 3]))
    return jnp.where(ids < par[LIVE], reach, 0)


def tap_moves(par):
    moves = []
    for a in range(3):
        for b in range(3):
            row = (a - 1) * par[DIL]
            moves.append((a, (b - 1) * par[DIL + 1] - row))
    return moves


def pack_edges(par, field, first, last, pick):
    lane = iota((1, 2 * ROWS), 1)
    near = lane % DMAX
    want = jnp.where(lane < ROWS, near, par[LIVE] - DMAX + near)
    place = (lane % ROWS) // DMAX
    rows = iota((ROWS, 2 * ROWS), 0)
    for kk in range(EDGE):
        hit = (rows == want) & (place == kk)
        pick[kk * ROWS:(kk + 1) * ROWS, :] = jnp.where(hit, 1.0, 0.0).astype(BF)

    def group(g, carry):
        lhs = jnp.concatenate([field[g * EDGE + kk] for kk in range(EDGE)], axis=1)
        out = jnp.dot(lhs, pick[...], preferred_element_type=F32).astype(BF)
        first[g] = out[:, :ROWS]
        last[g] = out[:, ROWS:]
        return carry

    lax.fori_loop(0, GROUPS, group, 0)


def shift_rows(par, field, left, right, top, bot, moved):
    lane = iota((1, 2 * ROWS), 1)
    move = jnp.where(lane < ROWS, -par[DIL], par[DIL])
    want = (lane % ROWS) + move
    rows = iota((ROWS, 2 * ROWS), 0)
    inner = jnp.where(rows == want, 1.0, 0.0).astype(BF)
    has_top = par[TILE] > 0
    has_bot = par[TILE] < par[LAST_TILE]
    top_want = jnp.where((want < 0) & has_top, want + DMAX, -1)
    low = want - par[LIVE]
    bot_want = jnp.where((low >= 0) & (low < DMAX) & has_bot, low, -1)
    has_left = par[DIAG] > 0
    has_right = par[DIAG] < par[LAST_DIAG]
    tops = top[...].reshape((GROUPS + 2) * CH, ROWS)
    bots = bot[...].reshape((GROUPS + 2) * CH, ROWS)

    def column(kk, carry):
        part = rows - kk * DMAX
        inside = (part >= 0) & (part < DMAX)
        part = jnp.where(inside, part, -2)
        upper = jnp.where(part == top_want, 1.0, 0.0).astype(BF)
        lower = jnp.where(part == bot_want, 1.0, 0.0).astype(BF)
        weight = jnp.concatenate([inner, upper, lower], axis=0)
        tiles = [left[kk]] + [field[g * EDGE + kk] for g in range(GROUPS)] + [right[kk]]
        lhs = jnp.concatenate([jnp.concatenate(tiles, axis=0), tops, bots], axis=1)
        out = jnp.dot(lhs, weight, preferred_element_type=F32)
        for g in range(GROUPS + 2):
            piece = out[g * CH:(g + 1) * CH]
            same = tiles[g]
            if g == 0:
                piece = jnp.where(has_left, piece, 0.0)
                same = jnp.where(has_left, same, jnp.zeros_like(same))
            if g == GROUPS + 1:
                piece = jnp.where(has_right, piece, 0.0)
                same = jnp.where(has_right, same, jnp.zeros_like(same))
            piece = piece.astype(BF)
            moved[0, g * EDGE + kk] = piece[:, :ROWS]
            moved[1, g * EDGE + kk] = same
            moved[2, g * EDGE + kk] = piece[:, ROWS:]
        return carry

    lax.fori_loop(0, EDGE, column, 0)


def prep_kernel(par, x_ref, g_ref, field, masked, first, last, x_t, g_t, pick):
    shape = (ROWS, COLS)
    keep = iota(shape, 1) + par[DIAG] * COLS < reach_of(par, iota(shape, 0))

    def channel(c, carry):
        x = jnp.where(keep, jnp.maximum(x_ref[c].astype(F32), 0.0), 0.0)
        g = jnp.where(keep, g_ref[c].astype(F32), 0.0)
        x_t[pl.ds(c, COLS, stride=CH), :] = x.T
        g_t[pl.ds(c, COLS, stride=CH), :] = g.T
        return carry

    lax.fori_loop(0, CH, channel, 0, unroll=2)

    def column(k, carry):
        at = pl.ds(pl.multiple_of(k * CH, CH), CH)
        field[k] = x_t[at, :].astype(BF)
        masked[k] = g_t[at, :].astype(BF)
        return carry

    lax.fori_loop(0, COLS, column, 0, unroll=4)
    pack_edges(par, field, first, last, pick)


def forward_kernel(par, field, left, right, top, bot, masked, weight,
                   grad_pre, first, last, total, moved, stack, acc, pick):
    shift_rows(par, field, left, right, top, bot, moved)
    moves = tap_moves(par)
    acc[...] = jnp.zeros_like(acc)
    used = (TAPS + 1) * CH
    stack[used:, :] = jnp.zeros((KPAD - used, STEP * ROWS), BF)

    def block(blk, carry):
        for j in range(STEP):
            k = blk * STEP + j
            lanes = slice(j * ROWS, (j + 1) * ROWS)
            for s, (a, shift) in enumerate(moves):
                stack[s * CH:(s + 1) * CH, lanes] = moved[a, EDGE + k + shift]
            stack[TAPS * CH:used, lanes] = masked[k]
        out = jnp.dot(weight[...], stack[...], preferred_element_type=F32)
        pre, back = out[:CH], out[CH:]
        grad = jnp.where(pre > 0, back, 0.0).astype(BF)
        lhs = jnp.concatenate([grad, stack[TAPS * CH:used, :]], axis=0)
        stack[TAPS * CH:used, :] = jnp.maximum(pre, 0.0).astype(BF)
        for j in range(STEP):
            grad_pre[blk * STEP + j] = grad[:, j * ROWS:(j + 1) * ROWS]
        acc[...] += lax.dot_general(lhs, stack[...], (((1,), (1,)), ((), ())),
                                    preferred_element_type=F32)
        return carry

    lax.fori_loop(0, COLS // STEP, block, 0)
    both = jnp.where(iota((CH, KPAD), 1) < TAPS * CH, acc[:CH], acc[CH:])
    for n in range(SHARES):
        if n < 2 * (CH // 8):
            at = (n // 2) * 8
            total[n] = both[at:at + 8, (n % 2) * 2 * ROWS:(n % 2 + 1) * 2 * ROWS]
        else:
            total[n] = jnp.zeros((8, 2 * ROWS), F32)
    pack_edges(par, grad_pre, first, last, pick)


def backward_kernel(par, field, left, right, top, bot, x_ref, g_ref, weight, out_ref,
                    moved, stack, spread):
    shift_rows(par, field, left, right, top, bot, moved)
    moves = tap_moves(par)
    used = TAPS * CH
    stack[used:, :] = jnp.zeros((KPAD - used, STEP * ROWS), BF)

    def block(blk, carry):
        for j in range(STEP):
            k = blk * STEP + j
            lanes = slice(j * ROWS, (j + 1) * ROWS)
            for s, (a, shift) in enumerate(moves):
                stack[s * CH:(s + 1) * CH, lanes] = moved[2 - a, EDGE + k - shift]
        out = jnp.dot(weight[...], stack[...], preferred_element_type=F32)
        for j in range(STEP):
            at = pl.ds(pl.multiple_of((blk * STEP + j) * CH, CH), CH)
            spread[at, :] = out[:, j * ROWS:(j + 1) * ROWS]
        return carry

    lax.fori_loop(0, COLS // STEP, block, 0)
    shape = (ROWS, COLS)
    ids = iota(shape, 0)
    keep = iota(shape, 1) + par[DIAG] * COLS < reach_of(par, ids)
    live = ids < par[LIVE]

    def channel(c, carry):
        part = spread[pl.ds(c, COLS, stride=CH), :].T
        x = x_ref[c].astype(F32)
        full = g_ref[c].astype(F32) + jnp.where(keep & (x > 0), part, 0.0)
        out_ref[c] = jnp.where(live, full, 0.0).astype(BF)
        return carry

    lax.fori_loop(0, CH, channel, 0, unroll=2)


def exchange_kernel(field, first, last, left, right, top, bot, send, recv):
    tile, diag = lax.axis_index("tiles"), lax.axis_index("diag")
    tiles, diags = lax.axis_size("tiles"), lax.axis_size("diag")
    up, down = lax.rem(tile + tiles - 1, tiles), lax.rem(tile + 1, tiles)
    lo, hi = lax.rem(diag + diags - 1, diags), lax.rem(diag + 1, diags)
    barrier = pltpu.get_barrier_semaphore()
    near = [(tile, lo), (tile, hi), (up, diag), (down, diag), (up, lo), (up, hi), (down, lo), (down, hi)]
    for device in near:
        pl.semaphore_signal(barrier, inc=1, device_id=device, device_id_type=MESH)
    pl.semaphore_wait(barrier, len(near))
    inner = pl.ds(1, GROUPS)
    plan = [
        (field.at[pl.ds(0, EDGE)], right, near[0]),
        (field.at[pl.ds(COLS - EDGE, EDGE)], left, near[1]),
        (first, bot.at[inner], near[2]),
        (last, top.at[inner], near[3]),
        (first.at[0], bot.at[GROUPS + 1], near[4]),
        (first.at[GROUPS - 1], bot.at[0], near[5]),
        (last.at[0], top.at[GROUPS + 1], near[6]),
        (last.at[GROUPS - 1], top.at[0], near[7]),
    ]
    copies = []
    for n, (src, dst, device) in enumerate(plan):
        copy = pltpu.make_async_remote_copy(src_ref=src, dst_ref=dst, send_sem=send.at[n], recv_sem=recv.at[n],
                                            device_id=device, device_id_type=MESH)
        copy.start()
        copies.append(copy)
    for copy in copies:
        copy.wait()


def sum_kernel(scale, part, conv_ref, mix_ref, near, far, done, send, recv, far_send, far_recv, out_send, out_recv):
    tile, diag = lax.axis_index("tiles"), lax.axis_index("diag")
    outer, other = lax.div(tile, SHARES), lax.rem(tile, SHARES)
    rank = outer * 4 + diag

    def friend(step):
        to = lax.rem(rank + step, SHARES)
        return to, (lax.div(to, 4) * SHARES + other, lax.rem(to, 4))

    def cousin(step):
        return (outer * SHARES + lax.rem(other + step, SHARES), diag)

    barrier = pltpu.get_barrier_semaphore()
    for step in range(1, SHARES):
        pl.semaphore_signal(barrier, inc=1, device_id=friend(step)[1], device_id_type=MESH)
        pl.semaphore_signal(barrier, inc=1, device_id=cousin(step), device_id_type=MESH)
    pl.semaphore_wait(barrier, 2 * (SHARES - 1))

    def first_copy(step):
        to, device = friend(step)
        return pltpu.make_async_remote_copy(
            src_ref=part.at[to], dst_ref=near.at[rank], send_sem=send.at[step], recv_sem=recv.at[step],
            device_id=device, device_id_type=MESH)

    def far_copy(step):
        return pltpu.make_async_remote_copy(
            src_ref=far.at[other], dst_ref=far.at[other], send_sem=far_send.at[step], recv_sem=far_recv.at[step],
            device_id=cousin(step), device_id_type=MESH)

    def out_copy(step):
        return pltpu.make_async_remote_copy(
            src_ref=done.at[rank], dst_ref=done.at[rank], send_sem=out_send.at[step], recv_sem=out_recv.at[step],
            device_id=friend(step)[1], device_id_type=MESH)

    steps = range(1, SHARES)
    for step in steps:
        first_copy(step).start()
    near[rank] = part[rank]
    for step in steps:
        first_copy(step).wait_recv()
    far[other] = jnp.sum(near[...], axis=0)
    for step in steps:
        far_copy(step).start()
    for step in steps:
        far_copy(step).wait_recv()
    done[rank] = jnp.sum(far[...], axis=0)
    for step in steps:
        out_copy(step).start()
    for step in steps:
        out_copy(step).wait_recv()
    for g in range(CH // 8):
        row = jnp.concatenate([done[2 * g], done[2 * g + 1]], axis=1) * scale
        for s in range(TAPS):
            conv_ref[s, 8 * g:8 * g + 8, :] = row[:, s * CH:(s + 1) * CH]
        mix_ref[8 * g:8 * g + 8, :] = row[:, TAPS * CH:(TAPS + 1) * CH]
    for step in steps:
        first_copy(step).wait_send()
        far_copy(step).wait_send()
        out_copy(step).wait_send()


def vmem_spec(count):
    return [pl.BlockSpec(memory_space=pltpu.VMEM)] * count


def local_call(kernel, outs, scratch, operands, flops):
    size = sum(math.prod(o.shape) * o.dtype.itemsize for o in operands + outs)
    return pl.pallas_call(
        kernel,
        out_shape=outs,
        in_specs=[pl.BlockSpec(memory_space=pltpu.SMEM)] + vmem_spec(len(operands) - 1),
        out_specs=vmem_spec(len(outs)),
        scratch_shapes=scratch,
        cost_estimate=pl.CostEstimate(flops=flops, bytes_accessed=size, transcendentals=0),
        compiler_params=pltpu.CompilerParams(vmem_limit_bytes=VMEM_LIMIT),
    )(*operands)


def exchange(field, first, last, number):
    shape = jax.ShapeDtypeStruct
    return pl.pallas_call(
        exchange_kernel,
        out_shape=[shape((EDGE, CH, ROWS), BF)] * 2 + [shape((GROUPS + 2, CH, ROWS), BF)] * 2,
        in_specs=[pl.BlockSpec(memory_space=pl.ANY)] * 3,
        out_specs=[pl.BlockSpec(memory_space=pl.ANY)] * 4,
        scratch_shapes=[pltpu.SemaphoreType.DMA((8,)), pltpu.SemaphoreType.DMA((8,))],
        compiler_params=pltpu.CompilerParams(collective_id=number, has_side_effects=True),
    )(field, first, last)


def sum_over_devices(part, scale):
    shape = jax.ShapeDtypeStruct
    slots = pltpu.VMEM((SHARES, 8, 2 * ROWS), F32)
    return pl.pallas_call(
        functools.partial(sum_kernel, scale),
        out_shape=[shape((TAPS, CH, CH), F32), shape((CH, CH), F32)],
        in_specs=vmem_spec(1),
        out_specs=vmem_spec(2),
        scratch_shapes=[slots] * 3 + [pltpu.SemaphoreType.DMA((SHARES,))] * 6,
        compiler_params=pltpu.CompilerParams(collective_id=2, has_side_effects=True),
    )(part)


def body(inputs, cotangent, conv_weight, mix_weight, counts, band_reach, dilation):
    shape = jax.ShapeDtypeStruct
    tiles, diags = lax.axis_size("tiles"), lax.axis_size("diag")
    place = [lax.axis_index("tiles"), lax.axis_index("diag"), tiles - 1, diags - 1]
    par = jnp.concatenate([counts * (ROWS // 4), band_reach, dilation, jnp.stack([jnp.int32(p) for p in place])])
    taps = conv_weight.transpose(1, 0, 2).reshape(CH, TAPS * CH)
    zeros = jnp.zeros((CH, CH), BF)
    forward_weight = jnp.concatenate([
        jnp.concatenate([taps, zeros], axis=1),
        jnp.concatenate([jnp.zeros_like(taps), mix_weight.T], axis=1)], axis=0)
    forward_weight = jnp.pad(forward_weight, ((0, 0), (0, KPAD - (TAPS + 1) * CH)))
    back_weight = jnp.pad(conv_weight.transpose(2, 0, 1).reshape(CH, TAPS * CH), ((0, 0), (0, KPAD - TAPS * CH)))

    field_shape = shape((COLS, CH, ROWS), BF)
    pack_shape = shape((GROUPS, CH, ROWS), BF)
    turned = pltpu.VMEM((COLS * CH, ROWS), F32)
    pick = pltpu.VMEM((EDGE * ROWS, 2 * ROWS), BF)
    moved = pltpu.VMEM((3, COLS + 2 * EDGE, CH, ROWS), BF)
    stack = pltpu.VMEM((KPAD, STEP * ROWS), BF)
    conv_flops = 2 * CH * CH * TAPS * ROWS * COLS

    field, masked, first, last = local_call(
        prep_kernel, [field_shape, field_shape, pack_shape, pack_shape], [turned, turned, pick],
        [par, inputs, cotangent], 0)
    left, right, top, bot = exchange(field, first, last, 0)
    grad_pre, first, last, part = local_call(
        forward_kernel, [field_shape, pack_shape, pack_shape, shape((SHARES, 8, 2 * ROWS), F32)],
        [moved, stack, pltpu.VMEM((2 * CH, KPAD), F32), pick],
        [par, field, left, right, top, bot, masked, forward_weight], 2 * conv_flops)
    left, right, top, bot = exchange(grad_pre, first, last, 1)
    cells = TPD * tiles * (ROWS // 4) * COLS * diags
    grad_conv, grad_mix = sum_over_devices(part, 1.0 / math.sqrt(cells))
    (grad_inputs,) = local_call(
        backward_kernel, [shape((CH, ROWS, COLS), BF)], [moved, stack, turned],
        [par, grad_pre, left, right, top, bot, inputs, cotangent, back_weight], conv_flops)
    return (grad_inputs, grad_conv, grad_mix)


def solution(mesh):
    in_specs = (
        P(None, "tiles", "diag"),
        P(None, "tiles", "diag"),
        P(),
        P(),
        P("tiles"),
        P("tiles"),
        P(),
    )
    out_specs = (P(None, "tiles", "diag"), P(), P())
    return jax.shard_map(body, mesh=mesh, in_specs=in_specs, out_specs=out_specs, check_vma=False)
```

time: 468 us -> 106 us (0.23); the launches traced: 461 us -> 106 us
  waiting for transfers between devices: 227 us -> 0 us
  Pallas kernels: 0 us -> 98.1 us
  blocking collectives: 78.8 us -> 0 us
  matrix products: 54.9 us -> 0 us
  starting transfers between devices: 26.2 us -> 0 us
  between operations: 26.5 us -> 1.34 us
  other arithmetic: 22 us -> 0.09 us
  local copies, waits for them, and re-layouts: 25.6 us -> 5.97 us
    psum x1 -> x0, waiting for transfers between devices: 220 us -> none  [body(): conv_sum, mix_sum = lax.psum((conv_part, mix_part), ('tiles', 'diag'))]
    pallas_call x0 -> x6, Pallas kernels: none -> 98.1 us  [the longest x3 49.8 us: local_call(): pl.pallas_call(kernel, out_shape=outs, in_specs=[pl.BlockSpec(memory_spac...]
    psum x1 -> x0, blocking collectives: 78.8 us -> none  [body(): conv_sum, mix_sum = lax.psum((conv_part, mix_part), ('tiles', 'diag'))]
    dot_general x29 -> x0, matrix products: 54.9 us -> none  [the longest x10 24.3 us: mix_back(): lax.dot_general(weight, field, (((0,), (0,)), ((), ())), preferred_elemen...]
    ppermute x8 -> x0, starting transfers between devices: 26.2 us -> none  [the longest x4 18.7 us: with_halo(): before = lax.ppermute(last, axis, up)]
    concatenate x4 -> x1, other arithmetic: 17.1 us -> 0.09 us  [body(): jnp.concatenate([jnp.concatenate([taps, zeros], axis=1), jnp.concatenate(...]
    slice x9 -> x0, local copies, waits for them, and re-layouts: 12.4 us -> none  [the longest x4 7.86 us: with_halo(): last = lax.slice_in_dim(value, length - width, length, axis=dim)]
    ppermute x4 -> x0, local copies, waits for them, and re-layouts: 8.54 us -> none  [the longest x2 5 us: with_halo(): after = lax.ppermute(initial, axis, down)]
  transfers between devices with their start and end apart: 9 -> 0, of which waited for: 3 -> 0; matrix products, arithmetic and copies ran while one was open for 6% -> 0% of each run, Pallas kernels for 0% -> 0%
where the time goes in v1:
time: 106 us
  Pallas kernels  98.1 us (93%)
  local copies, waits for them, and re-layouts  5.97 us (6%)
  between operations  1.34 us (1%)
    pallas_call x3, Pallas kernels, local_call(): pl.pallas_call(kernel, out_shape=outs, in_specs=[pl.BlockSpec(memory_spac...  49.8 us
    pallas_call x2, Pallas kernels, exchange(): pl.pallas_call(exchange_kernel, out_shape=[shape((EDGE, CH, ROWS), BF)] *...  26.4 us
    pallas_call x1, Pallas kernels, sum_over_devices(): pl.pallas_call(functools.partial(sum_kernel, scale), out_shape=[shape((TA...  21.8 us
    unnamed x7, local copies, waits for them, and re-layouts  3.08 us

profile of v1, /device:TPU:1, one launch (start us, length us, event | category | flops | bytes accessed | tf_op | source)
XLA Modules:
  0.0 105.5 jit_solution(12957121599608731379)
XLA Ops:
  1.3 1.3 %concatenate.12.par = s32[11]{0:T(128)} concatenate(s32[1]{0:T(128)S(6)} %mul.3, s32[4]{0:T(128)} %param.12, s32[2]{0:T(128)} %param.13, s32[1]{0:T(128)} %bitcast, s32[1]{0:T(128)} %bitcast.1, s32[1]{0:T(128)} %constant.6.clone.1, s32[1]{0:T(128)} %constant.18.clone.1), dimensions={0} | concatenate | bytes 88 | tf_op jit(solution)/shard_map/concatenate | solution.py:345
  2.6 10.1 %shard_map.94 = (bf16[128,48,128]{2,1,0:T(8,128)(2,1)}, bf16[128,48,128]{2,1,0:T(8,128)(2,1)}, bf16[8,48,128]{2,1,0:T(8,128)(2,1)}, bf16[8,48,128]{2,1,0:T(8,128)(2,1)}) custom-call(s32[11]{0:T(128)} %concatenate.12.par, bf16[48,128,128]{2,1,0:T(8,128)(2,1)} %x_ref.3, bf16[48,128,128]{2,1,0:T(8,128)(2,1)} %g_ref.3), custom_call_target="tpu_custom_call" | custom-call | bytes 6488108 | tf_op jit(solution)/shard_map/pallas_call | solution.py:305
  12.7 0.0 copy-start
  12.7 0.0 copy-start.1
  12.7 16.2 %shard_map.95 = (bf16[16,48,128]{2,1,0:T(8,128)(2,1)}, bf16[16,48,128]{2,1,0:T(8,128)(2,1)}, bf16[10,48,128]{2,1,0:T(8,128)(2,1)}, bf16[10,48,128]{2,1,0:T(8,128)(2,1)}) custom-call(bf16[128,48,128]{2,1,0:T(8,128)(2,1)} %get-tuple-element.21.field, bf16[8,48,128]{2,1,0:T(8,128)(2,1)} %get-tuple-element.22.first, bf16[8,48,128]{2,1,0:T(8,128)(2,1)} %get-tuple-element.23.last), custom_call_target="tpu_custom_call" | custom-call | tf_op jit(solution)/shard_map/pallas_call | solution.py:318
  28.9 0.0 copy-done
  28.9 0.1 copy.13
  29.0 0.1 copy.14
  29.1 0.0 copy-done.1
  29.1 0.1 copy.15
  29.2 0.1 fusion.2
  29.3 0.7 pad.10.weight
  30.0 22.3 %shard_map.96 = (bf16[128,48,128]{2,1,0:T(8,128)(2,1)}, bf16[8,48,128]{2,1,0:T(8,128)(2,1)}, bf16[8,48,128]{2,1,0:T(8,128)(2,1)}, f32[16,8,256]{2,1,0:T(8,128)}) custom-call(s32[11]{0:T(128)} %concatenate.12.par, bf16[128,48,128]{2,1,0:T(8,128)(2,1)} %get-tuple-element.21.field, bf16[16,48,128]{2,1,0:T(8,128)(2,1)} %get-tuple-element.24.left, ...), custom_call_target="tpu_custom_call" | custom-call | flops 1358954496 | bytes 5783596 | tf_op jit(solution)/shard_map/pallas_call | solution.py:305
  52.3 10.2 %shard_map.97 = (bf16[16,48,128]{2,1,0:T(8,128)(2,1)}, bf16[16,48,128]{2,1,0:T(8,128)(2,1)}, bf16[10,48,128]{2,1,0:T(8,128)(2,1)}, bf16[10,48,128]{2,1,0:T(8,128)(2,1)}) custom-call(bf16[128,48,128]{2,1,0:T(8,128)(2,1)} %get-tuple-element.29.field, bf16[8,48,128]{2,1,0:T(8,128)(2,1)} %get-tuple-element.30.first, bf16[8,48,128]{2,1,0:T(8,128)(2,1)} %get-tuple-element.31.last), custom_call_target="tpu_custom_call" | custom-call | tf_op jit(solution)/shard_map/pallas_call | solution.py:318
  62.5 0.1 copy.16
  62.6 0.6 pad.11.weight
  63.2 17.5 %shard_map.98 = bf16[48,128,128]{2,1,0:T(8,128)(2,1)} custom-call(s32[11]{0:T(128)} %concatenate.12.par, bf16[128,48,128]{2,1,0:T(8,128)(2,1)} %get-tuple-element.29.field, bf16[16,48,128]{2,1,0:T(8,128)(2,1)} %get-tuple-element.32.left, bf16[16,48,128]{2,1,0:T(8,128)(2,1)} %get-tuple-element.33.right, bf16[10,48,128]{2,1,0:T(8,128)(2,1)} %get-tuple-element.34.top, ...), custom_call_target="tpu_custom_call" | custom-call | flops 679477248 | bytes 6979628 | tf_op jit(solution)/shard_map/pallas_call | solution.py:305
  80.7 21.8 %shard_map.99 = (f32[9,48,48]{2,1,0:T(8,128)}, f32[48,48]{1,0:T(8,128)}) custom-call(f32[16,8,256]{2,1,0:T(8,128)} %get-tuple-element.36.part), custom_call_target="tpu_custom_call" | custom-call | tf_op jit(solution)/shard_map/pallas_call | solution.py:331
  102.5 1.6 %copy.20 = f32[9,48,48]{2,1,0:T(8,128)} copy(f32[9,48,48]{2,1,0:T(8,128)} %get-tuple-element.43) | data formatting | bytes 165888
  104.2 1.3 %copy.21 = f32[48,48]{1,0:T(8,128)} copy(f32[48,48]{1,0:T(8,128)} %get-tuple-element.44) | data formatting | bytes 18432
Async XLA Ops:
  12.7 16.2 %copy-start = (bf16[9,48,48]{2,1,0:T(8,128)(2,1)S(1)}, bf16[9,48,48]{2,1,0:T(8,128)(2,1)}, u32[]{:S(2)}) copy-start(bf16[9,48,48]{2,1,0:T(8,128)(2,1)} %param.9) | copy-start | bytes 124420
  12.7 16.5 %copy-start.1 = (bf16[48,48]{1,0:T(8,128)(2,1)S(1)}, bf16[48,48]{1,0:T(8,128)(2,1)}, u32[]{:S(2)}) copy-start(bf16[48,48]{1,0:T(8,128)(2,1)} %param.10) | copy-start | bytes 13828

commit v2 on v1

--- a/solution.py
+++ b/solution.py
@@ -45,27 +45,26 @@
     return moves
 
 
-def pack_edges(par, field, first, last, pick):
+def pack_edges(par, field, first, last):
     lane = iota((1, 2 * ROWS), 1)
     near = lane % DMAX
     want = jnp.where(lane < ROWS, near, par[LIVE] - DMAX + near)
-    place = (lane % ROWS) // DMAX
-    rows = iota((ROWS, 2 * ROWS), 0)
-    for kk in range(EDGE):
-        hit = (rows == want) & (place == kk)
-        pick[kk * ROWS:(kk + 1) * ROWS, :] = jnp.where(hit, 1.0, 0.0).astype(BF)
-
-    def group(g, carry):
-        lhs = jnp.concatenate([field[g * EDGE + kk] for kk in range(EDGE)], axis=1)
-        out = jnp.dot(lhs, pick[...], preferred_element_type=F32).astype(BF)
-        first[g] = out[:, :ROWS]
-        last[g] = out[:, ROWS:]
-        return carry
-
-    lax.fori_loop(0, GROUPS, group, 0)
+    place = jnp.where(lane < ROWS, (lane // DMAX + EDGE // 2) % EDGE, (lane - ROWS) // DMAX)
+    hit = jnp.where(iota((ROWS, 2 * ROWS), 0) == want, 1.0, 0.0)
+    out = jnp.zeros((GROUPS * CH, 2 * ROWS), F32)
+    for kk in range(0, EDGE, 2):
+        weight = jnp.concatenate([jnp.where(place == kk + n, hit, 0.0).astype(BF) for n in range(2)], axis=0)
+        lhs = jnp.concatenate(
+            [jnp.concatenate([field[g * EDGE + kk + n] for g in range(GROUPS)], axis=0) for n in range(2)], axis=1)
+        out += jnp.dot(lhs, weight, preferred_element_type=F32)
+    out = out.astype(BF)
+    for g in range(GROUPS):
+        first[g] = out[g * CH:(g + 1) * CH, :ROWS]
+        last[g] = out[g * CH:(g + 1) * CH, ROWS:]
 
 
 def shift_rows(par, field, left, right, top, bot, moved):
+    half = ROWS // 2
     lane = iota((1, 2 * ROWS), 1)
     move = jnp.where(lane < ROWS, -par[DIL], par[DIL])
     want = (lane % ROWS) + move
@@ -76,132 +75,181 @@
     top_want = jnp.where((want < 0) & has_top, want + DMAX, -1)
     low = want - par[LIVE]
     bot_want = jnp.where((low >= 0) & (low < DMAX) & has_bot, low, -1)
+    wants = [jnp.where(rows < half, top_want, bot_want), jnp.where(rows < half, bot_want, top_want)]
+    outers = [jnp.where(rows % DMAX == w, 1.0, 0.0) for w in wants]
+    place = (rows % half) // DMAX
     has_left = par[DIAG] > 0
     has_right = par[DIAG] < par[LAST_DIAG]
     tops = top[...].reshape((GROUPS + 2) * CH, ROWS)
     bots = bot[...].reshape((GROUPS + 2) * CH, ROWS)
-
-    def column(kk, carry):
-        part = rows - kk * DMAX
-        inside = (part >= 0) & (part < DMAX)
-        part = jnp.where(inside, part, -2)
-        upper = jnp.where(part == top_want, 1.0, 0.0).astype(BF)
-        lower = jnp.where(part == bot_want, 1.0, 0.0).astype(BF)
-        weight = jnp.concatenate([inner, upper, lower], axis=0)
-        tiles = [left[kk]] + [field[g * EDGE + kk] for g in range(GROUPS)] + [right[kk]]
-        lhs = jnp.concatenate([jnp.concatenate(tiles, axis=0), tops, bots], axis=1)
-        out = jnp.dot(lhs, weight, preferred_element_type=F32)
-        for g in range(GROUPS + 2):
-            piece = out[g * CH:(g + 1) * CH]
-            same = tiles[g]
-            if g == 0:
-                piece = jnp.where(has_left, piece, 0.0)
-                same = jnp.where(has_left, same, jnp.zeros_like(same))
-            if g == GROUPS + 1:
-                piece = jnp.where(has_right, piece, 0.0)
-                same = jnp.where(has_right, same, jnp.zeros_like(same))
-            piece = piece.astype(BF)
-            moved[0, g * EDGE + kk] = piece[:, :ROWS]
-            moved[1, g * EDGE + kk] = same
-            moved[2, g * EDGE + kk] = piece[:, ROWS:]
-        return carry
-
-    lax.fori_loop(0, EDGE, column, 0)
-
-
-def prep_kernel(par, x_ref, g_ref, field, masked, first, last, x_t, g_t, pick):
+    upper = iota(tops.shape, 1) < half
+    halos = [jnp.where(upper, tops, bots), jnp.where(upper, bots, tops)]
+
+    for part in range(2):
+        def column(at, carry):
+            kk = at + part * (EDGE // 2)
+            weight = jnp.concatenate([inner, jnp.where(place == at, outers[part], 0.0).astype(BF)], axis=0)
+            tiles = [left[kk]] + [field[g * EDGE + kk] for g in range(GROUPS)] + [right[kk]]
+            tiles[0] = jnp.where(has_left, tiles[0], jnp.zeros_like(tiles[0]))
+            tiles[-1] = jnp.where(has_right, tiles[-1], jnp.zeros_like(tiles[-1]))
+            lhs = jnp.concatenate([jnp.concatenate(tiles, axis=0), halos[part]], axis=1)
+            out = jnp.dot(lhs, weight, preferred_element_type=F32)
+            for g in range(GROUPS + 2):
+                piece = out[g * CH:(g + 1) * CH]
+                if g == 0:
+                    piece = jnp.where(has_left, piece, 0.0)
+                if g == GROUPS + 1:
+                    piece = jnp.where(has_right, piece, 0.0)
+                piece = piece.astype(BF)
+                moved[0, g * EDGE + kk] = piece[:, :ROWS]
+                moved[1, g * EDGE + kk] = tiles[g]
+                moved[2, g * EDGE + kk] = piece[:, ROWS:]
+            return carry
+
+        lax.fori_loop(0, EDGE // 2, column, 0)
+
+
+def pair(refs):
+    return jnp.concatenate(refs, axis=1)
+
+
+def eye():
+    return jnp.where(iota((ROWS, ROWS), 0) == iota((ROWS, ROWS), 1), 1.0, 0.0).astype(BF)
+
+
+def turn(one, value):
+    return lax.dot_general(one, value, (((1,), (1,)), ((), ())), preferred_element_type=F32)
+
+
+def turn_field(value, held, field):
+    one = eye()
+
+    def channels(step, carry):
+        c = step * 4
+        out = turn(one, jnp.concatenate([value(c + n) for n in range(4)], axis=0))
+        for n in range(4):
+            held[pl.ds(c + n, COLS, stride=CH), :] = out[:, n * ROWS:(n + 1) * ROWS]
+        return carry
+
+    lax.fori_loop(0, CH // 4, channels, 0, unroll=2)
+
+    def column(k, carry):
+        field[k] = held[pl.ds(pl.multiple_of(k * CH, CH), CH), :].astype(BF)
+        return carry
+
+    lax.fori_loop(0, COLS, column, 0, unroll=8)
+
+
+def kept_cells(par):
     shape = (ROWS, COLS)
-    keep = iota(shape, 1) + par[DIAG] * COLS < reach_of(par, iota(shape, 0))
-
-    def channel(c, carry):
-        x = jnp.where(keep, jnp.maximum(x_ref[c].astype(F32), 0.0), 0.0)
-        g = jnp.where(keep, g_ref[c].astype(F32), 0.0)
-        x_t[pl.ds(c, COLS, stride=CH), :] = x.T
-        g_t[pl.ds(c, COLS, stride=CH), :] = g.T
-        return carry
-
-    lax.fori_loop(0, CH, channel, 0, unroll=2)
-
-    def column(k, carry):
-        at = pl.ds(pl.multiple_of(k * CH, CH), CH)
-        field[k] = x_t[at, :].astype(BF)
-        masked[k] = g_t[at, :].astype(BF)
-        return carry
-
-    lax.fori_loop(0, COLS, column, 0, unroll=4)
-    pack_edges(par, field, first, last, pick)
-
-
-def forward_kernel(par, field, left, right, top, bot, masked, weight,
-                   grad_pre, first, last, total, moved, stack, acc, pick):
-    shift_rows(par, field, left, right, top, bot, moved)
+    return iota(shape, 1) + par[DIAG] * COLS < reach_of(par, iota(shape, 0))
+
+
+def prep_kernel(par, x_ref, g_ref, field, masked, first, last, held):
+    keep = jnp.where(kept_cells(par), 1.0, 0.0).astype(BF)
+    turn_field(lambda c: jnp.maximum(x_ref[c], jnp.zeros((), BF)) * keep, held, field)
+    pack_edges(par, field, first, last)
+    turn_field(lambda c: g_ref[c] * keep, held, masked)
+
+
+def conv_forward(par, moved, masked, weight, grad_pre, hidden):
+    moves = tap_moves(par)
+    used = (TAPS + 1) * CH
+    pad = jnp.zeros((KPAD - used, 2 * ROWS), BF)
+
+    def block(blk, carry):
+        for j in range(0, STEP, 2):
+            k = blk * STEP + j
+            tiles = [pair([moved[a, EDGE + k + n + shift] for n in range(2)]) for a, shift in moves]
+            tiles += [pair([masked[k], masked[k + 1]]), pad]
+            out = jnp.dot(weight[...], jnp.concatenate(tiles, axis=0), preferred_element_type=F32)
+            pre, back = out[:CH], out[CH:]
+            grad = jnp.where(pre > 0, back, 0.0).astype(BF)
+            act = jnp.maximum(pre, 0.0).astype(BF)
+            for n in range(2):
+                grad_pre[k + n] = grad[:, n * ROWS:(n + 1) * ROWS]
+                hidden[k + n] = act[:, n * ROWS:(n + 1) * ROWS]
+        return carry
+
+    lax.fori_loop(0, COLS // STEP, block, 0)
+
+
+def kernel_grads(par, moved, masked, grad_pre, hidden, acc):
     moves = tap_moves(par)
     acc[...] = jnp.zeros_like(acc)
-    used = (TAPS + 1) * CH
-    stack[used:, :] = jnp.zeros((KPAD - used, STEP * ROWS), BF)
 
     def block(blk, carry):
-        for j in range(STEP):
-            k = blk * STEP + j
-            lanes = slice(j * ROWS, (j + 1) * ROWS)
-            for s, (a, shift) in enumerate(moves):
-                stack[s * CH:(s + 1) * CH, lanes] = moved[a, EDGE + k + shift]
-            stack[TAPS * CH:used, lanes] = masked[k]
-        out = jnp.dot(weight[...], stack[...], preferred_element_type=F32)
-        pre, back = out[:CH], out[CH:]
-        grad = jnp.where(pre > 0, back, 0.0).astype(BF)
-        lhs = jnp.concatenate([grad, stack[TAPS * CH:used, :]], axis=0)
-        stack[TAPS * CH:used, :] = jnp.maximum(pre, 0.0).astype(BF)
-        for j in range(STEP):
-            grad_pre[blk * STEP + j] = grad[:, j * ROWS:(j + 1) * ROWS]
-        acc[...] += lax.dot_general(lhs, stack[...], (((1,), (1,)), ((), ())),
-                                    preferred_element_type=F32)
+        ks = [blk * STEP + j for j in range(STEP)]
+        tiles = [pair([moved[a, EDGE + k + shift] for k in ks]) for a, shift in moves]
+        lhs = jnp.concatenate(tiles + [pair([hidden[k] for k in ks])], axis=0)
+        rhs = jnp.concatenate([pair([grad_pre[k] for k in ks]), pair([masked[k] for k in ks])], axis=0)
+        acc[:, :2 * CH] += lax.dot_general(lhs, rhs, (((1,), (1,)), ((), ())), preferred_element_type=F32)
         return carry
 
     lax.fori_loop(0, COLS // STEP, block, 0)
-    both = jnp.where(iota((CH, KPAD), 1) < TAPS * CH, acc[:CH], acc[CH:])
+
+
+def share_out(acc, total):
+    flat = acc[...].T
+    both = jnp.where(iota((CH, (TAPS + 1) * CH), 1) < TAPS * CH, flat[:CH], flat[CH:2 * CH])
+    both = jnp.concatenate([both, jnp.zeros((CH, KPAD - (TAPS + 1) * CH), F32)], axis=1)
     for n in range(SHARES):
         if n < 2 * (CH // 8):
             at = (n // 2) * 8
             total[n] = both[at:at + 8, (n % 2) * 2 * ROWS:(n % 2 + 1) * 2 * ROWS]
         else:
             total[n] = jnp.zeros((8, 2 * ROWS), F32)
-    pack_edges(par, grad_pre, first, last, pick)
-
-
-def backward_kernel(par, field, left, right, top, bot, x_ref, g_ref, weight, out_ref,
-                    moved, stack, spread):
+
+
+def forward_kernel(par, field, left, right, top, bot, masked, weight,
+                   grad_pre, first, last, total, moved, hidden, acc):
     shift_rows(par, field, left, right, top, bot, moved)
+    conv_forward(par, moved, masked, weight, grad_pre, hidden)
+    pack_edges(par, grad_pre, first, last)
+    kernel_grads(par, moved, masked, grad_pre, hidden, acc)
+    share_out(acc, total)
+
+
+def conv_back(par, moved, weight, spread):
     moves = tap_moves(par)
-    used = TAPS * CH
-    stack[used:, :] = jnp.zeros((KPAD - used, STEP * ROWS), BF)
+    pad = jnp.zeros((KPAD - TAPS * CH, 2 * ROWS), BF)
 
     def block(blk, carry):
-        for j in range(STEP):
+        for j in range(0, STEP, 2):
             k = blk * STEP + j
-            lanes = slice(j * ROWS, (j + 1) * ROWS)
-            for s, (a, shift) in enumerate(moves):
-                stack[s * CH:(s + 1) * CH, lanes] = moved[2 - a, EDGE + k - shift]
-        out = jnp.dot(weight[...], stack[...], preferred_element_type=F32)
-        for j in range(STEP):
-            at = pl.ds(pl.multiple_of((blk * STEP + j) * CH, CH), CH)
-            spread[at, :] = out[:, j * ROWS:(j + 1) * ROWS]
+            tiles = [pair([moved[2 - a, EDGE + k + n - shift] for n in range(2)]) for a, shift in moves]
+            out = jnp.dot(weight[...], jnp.concatenate(tiles + [pad], axis=0), preferred_element_type=F32)
+            for n in range(2):
+                at = pl.ds(pl.multiple_of((k + n) * CH, CH), CH)
+                spread[at, :] = out[:, n * ROWS:(n + 1) * ROWS]
         return carry
 
     lax.fori_loop(0, COLS // STEP, block, 0)
-    shape = (ROWS, COLS)
-    ids = iota(shape, 0)
-    keep = iota(shape, 1) + par[DIAG] * COLS < reach_of(par, ids)
-    live = ids < par[LIVE]
-
-    def channel(c, carry):
-        part = spread[pl.ds(c, COLS, stride=CH), :].T
-        x = x_ref[c].astype(F32)
-        full = g_ref[c].astype(F32) + jnp.where(keep & (x > 0), part, 0.0)
-        out_ref[c] = jnp.where(live, full, 0.0).astype(BF)
-        return carry
-
-    lax.fori_loop(0, CH, channel, 0, unroll=2)
+
+
+def finish(par, x_ref, g_ref, spread, out_ref):
+    keep = kept_cells(par)
+    live = iota((ROWS, COLS), 0) < par[LIVE]
+    one = eye()
+
+    def channels(step, carry):
+        c = step * 4
+        parts = [spread[pl.ds(c + n, COLS, stride=CH), :].astype(BF) for n in range(4)]
+        out = turn(one, jnp.concatenate(parts, axis=0))
+        for n in range(4):
+            part = out[:, n * ROWS:(n + 1) * ROWS]
+            x = x_ref[c + n].astype(F32)
+            full = g_ref[c + n].astype(F32) + jnp.where(keep & (x > 0), part, 0.0)
+            out_ref[c + n] = jnp.where(live, full, 0.0).astype(BF)
+        return carry
+
+    lax.fori_loop(0, CH // 4, channels, 0, unroll=2)
+
+
+def backward_kernel(par, field, left, right, top, bot, x_ref, g_ref, weight, out_ref, moved, spread):
+    shift_rows(par, field, left, right, top, bot, moved)
+    conv_back(par, moved, weight, spread)
+    finish(par, x_ref, g_ref, spread, out_ref)
 
 
 def exchange_kernel(field, first, last, left, right, top, bot, send, recv):
@@ -354,24 +402,23 @@
     field_shape = shape((COLS, CH, ROWS), BF)
     pack_shape = shape((GROUPS, CH, ROWS), BF)
     turned = pltpu.VMEM((COLS * CH, ROWS), F32)
-    pick = pltpu.VMEM((EDGE * ROWS, 2 * ROWS), BF)
+    hidden = pltpu.VMEM((COLS, CH, ROWS), BF)
     moved = pltpu.VMEM((3, COLS + 2 * EDGE, CH, ROWS), BF)
-    stack = pltpu.VMEM((KPAD, STEP * ROWS), BF)
     conv_flops = 2 * CH * CH * TAPS * ROWS * COLS
 
     field, masked, first, last = local_call(
-        prep_kernel, [field_shape, field_shape, pack_shape, pack_shape], [turned, turned, pick],
+        prep_kernel, [field_shape, field_shape, pack_shape, pack_shape], [turned],
         [par, inputs, cotangent], 0)
     left, right, top, bot = exchange(field, first, last, 0)
     grad_pre, first, last, part = local_call(
         forward_kernel, [field_shape, pack_shape, pack_shape, shape((SHARES, 8, 2 * ROWS), F32)],
-        [moved, stack, pltpu.VMEM((2 * CH, KPAD), F32), pick],
+        [moved, hidden, pltpu.VMEM(((TAPS + 1) * CH, ROWS), F32)],
         [par, field, left, right, top, bot, masked, forward_weight], 2 * conv_flops)
     left, right, top, bot = exchange(grad_pre, first, last, 1)
     cells = TPD * tiles * (ROWS // 4) * COLS * diags
     grad_conv, grad_mix = sum_over_devices(part, 1.0 / math.sqrt(cells))
     (grad_inputs,) = local_call(
-        backward_kernel, [shape((CH, ROWS, COLS), BF)], [moved, stack, turned],
+        backward_kernel, [shape((CH, ROWS, COLS), BF)], [moved, turned],
         [par, grad_pre, left, right, top, bot, inputs, cotangent, back_weight], conv_flops)
     return (grad_inputs, grad_conv, grad_mix)
 

time: 106 us -> 97.5 us (0.920)
  Pallas kernels: 98.1 us -> 89.9 us
    pallas_call x3, Pallas kernels: 49.8 us -> 41.6 us  [local_call(): pl.pallas_call(kernel, out_shape=outs, in_specs=[pl.BlockSpec(memory_spac...]
where the time goes in v2:
time: 97.5 us; the launch traced here: 97.3 us
  Pallas kernels  89.9 us (92%)
  local copies, waits for them, and re-layouts  5.97 us (6%)
  between operations  1.34 us (1%)
    pallas_call x3, Pallas kernels, local_call(): pl.pallas_call(kernel, out_shape=outs, in_specs=[pl.BlockSpec(memory_spac...  41.6 us
    pallas_call x2, Pallas kernels, exchange(): pl.pallas_call(exchange_kernel, out_shape=[shape((EDGE, CH, ROWS), BF)] *...  26.4 us
    pallas_call x1, Pallas kernels, sum_over_devices(): pl.pallas_call(functools.partial(sum_kernel, scale), out_shape=[shape((TA...  21.9 us
    unnamed x7, local copies, waits for them, and re-layouts  3.08 us

profile of v2, /device:TPU:1, one launch (start us, length us, event | category | flops | bytes accessed | tf_op | source)
XLA Modules:
  0.0 97.3 jit_solution(10544626241550474696)
XLA Ops:
  1.3 1.3 %concatenate.12.par = s32[11]{0:T(128)} concatenate(s32[1]{0:T(128)S(6)} %mul.3, s32[4]{0:T(128)} %param.12, s32[2]{0:T(128)} %param.13, s32[1]{0:T(128)} %bitcast, s32[1]{0:T(128)} %bitcast.1, s32[1]{0:T(128)} %constant.6.clone.1, s32[1]{0:T(128)} %constant.18.clone.1), dimensions={0} | concatenate | bytes 88 | tf_op jit(solution)/shard_map/concatenate | solution.py:393
  2.6 8.4 %shard_map.94 = (bf16[128,48,128]{2,1,0:T(8,128)(2,1)}, bf16[128,48,128]{2,1,0:T(8,128)(2,1)}, bf16[8,48,128]{2,1,0:T(8,128)(2,1)}, bf16[8,48,128]{2,1,0:T(8,128)(2,1)}) custom-call(s32[11]{0:T(128)} %concatenate.12.par, bf16[48,128,128]{2,1,0:T(8,128)(2,1)} %x_ref.3, bf16[48,128,128]{2,1,0:T(8,128)(2,1)} %g_ref.3), custom_call_target="tpu_custom_call" | custom-call | bytes 6488108 | tf_op jit(solution)/shard_map/pallas_call | solution.py:353
  10.9 0.0 copy-start
  10.9 0.0 copy-start.1
  10.9 16.2 %shard_map.95 = (bf16[16,48,128]{2,1,0:T(8,128)(2,1)}, bf16[16,48,128]{2,1,0:T(8,128)(2,1)}, bf16[10,48,128]{2,1,0:T(8,128)(2,1)}, bf16[10,48,128]{2,1,0:T(8,128)(2,1)}) custom-call(bf16[128,48,128]{2,1,0:T(8,128)(2,1)} %get-tuple-element.21.field, bf16[8,48,128]{2,1,0:T(8,128)(2,1)} %get-tuple-element.22.first, bf16[8,48,128]{2,1,0:T(8,128)(2,1)} %get-tuple-element.23.last), custom_call_target="tpu_custom_call" | custom-call | tf_op jit(solution)/shard_map/pallas_call | solution.py:366
  27.2 0.0 copy-done
  27.2 0.1 copy.13
  27.3 0.1 copy.14
  27.4 0.0 copy-done.1
  27.4 0.1 copy.15
  27.5 0.1 fusion.2
  27.6 0.7 pad.10.weight
  28.2 19.1 %shard_map.96 = (bf16[128,48,128]{2,1,0:T(8,128)(2,1)}, bf16[8,48,128]{2,1,0:T(8,128)(2,1)}, bf16[8,48,128]{2,1,0:T(8,128)(2,1)}, f32[16,8,256]{2,1,0:T(8,128)}) custom-call(s32[11]{0:T(128)} %concatenate.12.par, bf16[128,48,128]{2,1,0:T(8,128)(2,1)} %get-tuple-element.21.field, bf16[16,48,128]{2,1,0:T(8,128)(2,1)} %get-tuple-element.24.left, ...), custom_call_target="tpu_custom_call" | custom-call | flops 1358954496 | bytes 5783596 | tf_op jit(solution)/shard_map/pallas_call | solution.py:353
  47.4 10.2 %shard_map.97 = (bf16[16,48,128]{2,1,0:T(8,128)(2,1)}, bf16[16,48,128]{2,1,0:T(8,128)(2,1)}, bf16[10,48,128]{2,1,0:T(8,128)(2,1)}, bf16[10,48,128]{2,1,0:T(8,128)(2,1)}) custom-call(bf16[128,48,128]{2,1,0:T(8,128)(2,1)} %get-tuple-element.29.field, bf16[8,48,128]{2,1,0:T(8,128)(2,1)} %get-tuple-element.30.first, bf16[8,48,128]{2,1,0:T(8,128)(2,1)} %get-tuple-element.31.last), custom_call_target="tpu_custom_call" | custom-call | tf_op jit(solution)/shard_map/pallas_call | solution.py:366
  57.6 0.1 copy.16
  57.7 0.6 pad.11.weight
  58.3 14.2 %shard_map.98 = bf16[48,128,128]{2,1,0:T(8,128)(2,1)} custom-call(s32[11]{0:T(128)} %concatenate.12.par, bf16[128,48,128]{2,1,0:T(8,128)(2,1)} %get-tuple-element.29.field, bf16[16,48,128]{2,1,0:T(8,128)(2,1)} %get-tuple-element.32.left, bf16[16,48,128]{2,1,0:T(8,128)(2,1)} %get-tuple-element.33.right, bf16[10,48,128]{2,1,0:T(8,128)(2,1)} %get-tuple-element.34.top, ...), custom_call_target="tpu_custom_call" | custom-call | flops 679477248 | bytes 6979628 | tf_op jit(solution)/shard_map/pallas_call | solution.py:353
  72.5 21.9 %shard_map.99 = (f32[9,48,48]{2,1,0:T(8,128)}, f32[48,48]{1,0:T(8,128)}) custom-call(f32[16,8,256]{2,1,0:T(8,128)} %get-tuple-element.36.part), custom_call_target="tpu_custom_call" | custom-call | tf_op jit(solution)/shard_map/pallas_call | solution.py:379
  94.3 1.6 %copy.20 = f32[9,48,48]{2,1,0:T(8,128)} copy(f32[9,48,48]{2,1,0:T(8,128)} %get-tuple-element.43) | data formatting | bytes 165888
  96.0 1.3 %copy.21 = f32[48,48]{1,0:T(8,128)} copy(f32[48,48]{1,0:T(8,128)} %get-tuple-element.44) | data formatting | bytes 18432
Async XLA Ops:
  10.9 16.2 %copy-start = (bf16[9,48,48]{2,1,0:T(8,128)(2,1)S(1)}, bf16[9,48,48]{2,1,0:T(8,128)(2,1)}, u32[]{:S(2)}) copy-start(bf16[9,48,48]{2,1,0:T(8,128)(2,1)} %param.9) | copy-start | bytes 124420
  10.9 16.5 %copy-start.1 = (bf16[48,48]{1,0:T(8,128)(2,1)S(1)}, bf16[48,48]{1,0:T(8,128)(2,1)}, u32[]{:S(2)}) copy-start(bf16[48,48]{1,0:T(8,128)(2,1)} %param.10) | copy-start | bytes 13828

commit v3 on v2

v3 whole, which is shorter than its diff:
```python
import functools
import math

import jax
import jax.numpy as jnp
from jax import lax
from jax.experimental import pallas as pl
from jax.experimental.pallas import tpu as pltpu
from jax.sharding import PartitionSpec as P

MESH = pl.DeviceIdType.MESH
TPD = 2
DMAX = 8
CH = 48
ROWS = 128
COLS = 128
EDGE = 2 * DMAX
GROUPS = COLS // EDGE
STEP = 8
TAPS = 9
KPAD = 512
VMEM_LIMIT = 56 * 1024 * 1024
BF = jnp.bfloat16
F32 = jnp.float32
LIVE, REACH, DIL, TILE, DIAG, LAST_TILE, LAST_DIAG = 0, 1, 5, 7, 8, 9, 10
TURN = 56
BACK = 136
PIECES = 16
MOVES = 8


def iota(shape, dim):
    return lax.broadcasted_iota(jnp.int32, shape, dim)


def reach_of(par, ids):
    reach = jnp.where(ids < 64, jnp.where(ids < 32, par[REACH], par[REACH + 1]),
                      jnp.where(ids < 96, par[REACH + 2], par[REACH + 3]))
    return jnp.where(ids < par[LIVE], reach, 0)


def tap_moves(par):
    moves = []
    for a in range(3):
        for b in range(3):
            row = (a - 1) * par[DIL]
            moves.append((a, (b - 1) * par[DIL + 1] - row))
    return moves


def pack_edges(par, field, first, last):
    lane = iota((1, 2 * ROWS), 1)
    near = lane % DMAX
    want = jnp.where(lane < ROWS, near, par[LIVE] - DMAX + near)
    place = jnp.where(lane < ROWS, (lane // DMAX + EDGE // 2) % EDGE, (lane - ROWS) // DMAX)
    hit = jnp.where(iota((ROWS, 2 * ROWS), 0) == want, 1.0, 0.0)
    out = jnp.zeros((GROUPS * CH, 2 * ROWS), F32)
    for kk in range(0, EDGE, 2):
        weight = jnp.concatenate([jnp.where(place == kk + n, hit, 0.0).astype(BF) for n in range(2)], axis=0)
        lhs = jnp.concatenate(
            [jnp.concatenate([field[g * EDGE + kk + n] for g in range(GROUPS)], axis=0) for n in range(2)], axis=1)
        out += jnp.dot(lhs, weight, preferred_element_type=F32)
    out = out.astype(BF)
    for g in range(GROUPS):
        first[g] = out[g * CH:(g + 1) * CH, :ROWS]
        last[g] = out[g * CH:(g + 1) * CH, ROWS:]


def shift_rows(par, field, left, right, top, bot, moved):
    half = ROWS // 2
    lane = iota((1, 2 * ROWS), 1)
    move = jnp.where(lane < ROWS, -par[DIL], par[DIL])
    want = (lane % ROWS) + move
    rows = iota((ROWS, 2 * ROWS), 0)
    inner = jnp.where(rows == want, 1.0, 0.0).astype(BF)
    has_top = par[TILE] > 0
    has_bot = par[TILE] < par[LAST_TILE]
    top_want = jnp.where((want < 0) & has_top, want + DMAX, -1)
    low = want - par[LIVE]
    bot_want = jnp.where((low >= 0) & (low < DMAX) & has_bot, low, -1)
    wants = [jnp.where(rows < half, top_want, bot_want), jnp.where(rows < half, bot_want, top_want)]
    outers = [jnp.where(rows % DMAX == w, 1.0, 0.0) for w in wants]
    place = (rows % half) // DMAX
    has_left = par[DIAG] > 0
    has_right = par[DIAG] < par[LAST_DIAG]
    tops = top[...].reshape((GROUPS + 2) * CH, ROWS)
    bots = bot[...].reshape((GROUPS + 2) * CH, ROWS)
    upper = iota(tops.shape, 1) < half
    halos = [jnp.where(upper, tops, bots), jnp.where(upper, bots, tops)]

    for part in range(2):
        def column(at, carry):
            kk = at + part * (EDGE // 2)
            weight = jnp.concatenate([inner, jnp.where(place == at, outers[part], 0.0).astype(BF)], axis=0)
            tiles = [left[kk]] + [field[g * EDGE + kk] for g in range(GROUPS)] + [right[kk]]
            tiles[0] = jnp.where(has_left, tiles[0], jnp.zeros_like(tiles[0]))
            tiles[-1] = jnp.where(has_right, tiles[-1], jnp.zeros_like(tiles[-1]))
            lhs = jnp.concatenate([jnp.concatenate(tiles, axis=0), halos[part]], axis=1)
            out = jnp.dot(lhs, weight, preferred_element_type=F32)
            for g in range(GROUPS + 2):
                piece = out[g * CH:(g + 1) * CH]
                if g == 0:
                    piece = jnp.where(has_left, piece, 0.0)
                if g == GROUPS + 1:
                    piece = jnp.where(has_right, piece, 0.0)
                piece = piece.astype(BF)
                moved[0, g * EDGE + kk] = piece[:, :ROWS]
                moved[1, g * EDGE + kk] = tiles[g]
                moved[2, g * EDGE + kk] = piece[:, ROWS:]
            return carry

        lax.fori_loop(0, EDGE // 2, column, 0, unroll=2)


def pair(refs):
    return jnp.concatenate(refs, axis=1)


def eye():
    return jnp.where(iota((ROWS, ROWS), 0) == iota((ROWS, ROWS), 1), 1.0, 0.0).astype(BF)


def turn(one, value):
    return lax.dot_general(one, value, (((1,), (1,)), ((), ())), preferred_element_type=F32)


def turn_field(value, held, field):
    one = eye()

    def channels(step, carry):
        c = step * 4
        out = turn(one, jnp.concatenate([value(c + n) for n in range(4)], axis=0))
        for n in range(4):
            held[pl.ds(c + n, COLS, stride=TURN), :] = out[:, n * ROWS:(n + 1) * ROWS]
        return carry

    lax.fori_loop(0, CH // 4, channels, 0, unroll=2)

    def column(k, carry):
        field[k] = held[pl.ds(pl.multiple_of(k * TURN, 8), CH), :].astype(BF)
        return carry

    lax.fori_loop(0, COLS, column, 0, unroll=8)


def kept_cells(par):
    shape = (ROWS, COLS)
    return iota(shape, 1) + par[DIAG] * COLS < reach_of(par, iota(shape, 0))


def conv_forward(par, blocks, moved, masked, weight, grad_pre, hidden):
    moves = tap_moves(par)
    used = (TAPS + 1) * CH
    pad = jnp.zeros((KPAD - used, 2 * ROWS), BF)
    count, number = blocks

    def block(at, carry):
        for j in range(0, STEP, 2):
            k = number(at) * STEP + j
            tiles = [pair([moved[a, EDGE + k + n + shift] for n in range(2)]) for a, shift in moves]
            tiles += [pair([masked[k], masked[k + 1]]), pad]
            out = jnp.dot(weight[...], jnp.concatenate(tiles, axis=0), preferred_element_type=F32)
            pre, back = out[:CH], out[CH:]
            grad = jnp.where(pre > 0, back, 0.0).astype(BF)
            act = jnp.maximum(pre, 0.0).astype(BF)
            for n in range(2):
                grad_pre[k + n] = grad[:, n * ROWS:(n + 1) * ROWS]
                hidden[k + n] = act[:, n * ROWS:(n + 1) * ROWS]
        return carry

    lax.fori_loop(0, count, block, 0, unroll=4)


def kernel_grads(par, moved, masked, grad_pre, hidden, acc):
    moves = tap_moves(par)
    acc[...] = jnp.zeros_like(acc)

    def block(blk, carry):
        ks = [blk * STEP + j for j in range(STEP)]
        tiles = [pair([moved[a, EDGE + k + shift] for k in ks]) for a, shift in moves]
        lhs = jnp.concatenate(tiles + [pair([hidden[k] for k in ks])], axis=0)
        rhs = jnp.concatenate([pair([grad_pre[k] for k in ks]), pair([masked[k] for k in ks])], axis=0)
        acc[:, :2 * CH] += lax.dot_general(lhs, rhs, (((1,), (1,)), ((), ())), preferred_element_type=F32)
        return carry

    lax.fori_loop(0, COLS // STEP, block, 0, unroll=2)


def share_out(acc, part):
    flat = acc[...].T
    both = jnp.where(iota((CH, (TAPS + 1) * CH), 1) < TAPS * CH, flat[:CH], flat[CH:2 * CH])
    both = jnp.concatenate([both, jnp.zeros((CH, KPAD - (TAPS + 1) * CH), F32)], axis=1)
    per = part.shape[1]
    for n in range(PIECES):
        at, half = (n // 2) * 8, (n % 2) * 2 * ROWS
        piece = both[at:at + 8, half:half + 2 * ROWS] if at < CH else jnp.zeros((8, 2 * ROWS), F32)
        part[n // per, n % per] = piece


def place_weights(conv, mix, forward, backward):
    shape = (CH, KPAD)
    gap = iota(shape, 1) - iota(shape, 0)
    taps = jnp.zeros(shape, F32)
    back = jnp.zeros(shape, F32)
    for s in range(TAPS):
        put = jnp.where(gap == s * CH, 1.0, 0.0).astype(BF)
        taps += jnp.dot(conv[s], put, preferred_element_type=F32)
        back += lax.dot_general(conv[s], put, (((0,), (0,)), ((), ())), preferred_element_type=F32)
    put = jnp.where(gap == TAPS * CH, 1.0, 0.0).astype(BF)
    mixed = lax.dot_general(mix[...], put, (((0,), (0,)), ((), ())), preferred_element_type=F32)
    forward[...] = jnp.concatenate([taps, mixed], axis=0).astype(BF)
    backward[...] = back.astype(BF)


def conv_back(par, first, count, moved, weight, spread):
    moves = tap_moves(par)
    pad = jnp.zeros((KPAD - TAPS * CH, 2 * ROWS), BF)

    def block(blk, carry):
        for j in range(0, STEP, 2):
            k = blk * STEP + j
            tiles = [pair([moved[2 - a, EDGE + k + n - shift] for n in range(2)]) for a, shift in moves]
            out = jnp.dot(weight[...], jnp.concatenate(tiles + [pad], axis=0), preferred_element_type=F32)
            for n in range(2):
                spread[pl.ds(k + n, CH, stride=BACK), :] = out[:, n * ROWS:(n + 1) * ROWS]
        return carry

    lax.fori_loop(first, first + count, block, 0, unroll=4)


def finish(par, x_ref, g_ref, spread, out_hbm, sems):
    keep = kept_cells(par)
    live = iota((ROWS, COLS), 0) < par[LIVE]
    one = eye()

    def channels(step, carry):
        c = step * 4
        parts = [spread[pl.ds(pl.multiple_of((c + n) * BACK, 8), COLS), :].astype(BF) for n in range(4)]
        out = turn(one, jnp.concatenate(parts, axis=0))
        for n in range(4):
            part = out[:, n * ROWS:(n + 1) * ROWS]
            x = x_ref[c + n].astype(F32)
            full = g_ref[c + n].astype(F32) + jnp.where(keep & (x > 0), part, 0.0)
            x_ref[c + n] = jnp.where(live, full, 0.0).astype(BF)
        chunk(step).start()
        return carry

    def chunk(step):
        at = pl.ds(step * 4, 4)
        return pltpu.make_async_copy(x_ref.at[at], out_hbm.at[at], sems.at[step])

    def end(step, carry):
        chunk(step).wait()
        return carry

    lax.fori_loop(0, CH // 4, channels, 0, unroll=2)
    return lambda: lax.fori_loop(0, CH // 4, end, 0)


def remote(src, dst, send, recv, device):
    return pltpu.make_async_remote_copy(src_ref=src, dst_ref=dst, send_sem=send, recv_sem=recv,
                                        device_id=device, device_id_type=MESH)


def neighbours():
    tile, diag = lax.axis_index("tiles"), lax.axis_index("diag")
    tiles, diags = lax.axis_size("tiles"), lax.axis_size("diag")
    up, down = lax.rem(tile + tiles - 1, tiles), lax.rem(tile + 1, tiles)
    lo, hi = lax.rem(diag + diags - 1, diags), lax.rem(diag + 1, diags)
    return [(tile, lo), (tile, hi), (up, diag), (down, diag), (up, lo), (up, hi), (down, lo), (down, hi)]


def halo_copies(near, field, first, last, left, right, top, bot, send, recv):
    inner = pl.ds(1, GROUPS)
    plan = [
        (field.at[pl.ds(0, EDGE)], right),
        (field.at[pl.ds(COLS - EDGE, EDGE)], left),
        (first, bot.at[inner]),
        (last, top.at[inner]),
        (first.at[0], bot.at[GROUPS + 1]),
        (first.at[GROUPS - 1], bot.at[0]),
        (last.at[0], top.at[GROUPS + 1]),
        (last.at[GROUPS - 1], top.at[0]),
    ]
    return [remote(src, dst, send.at[n], recv.at[n], near[n]) for n, (src, dst) in enumerate(plan)]


def everything(inner, counts, reach, dilation, x_hbm, g_hbm, conv, mix, out_hbm, sum_ref,
               x_ref, g_ref, field, masked, grad_pre, hidden, moved, held, spread, acc, forward, backward,
               first1, last1, left1, right1, top1, bot1, first2, last2, left2, right2, top2, bot2,
               part, parts_in, far, done, load, leave, send1, recv1, send2, recv2, send3, recv3, send4, recv4, send5, recv5):
    tile, diag = lax.axis_index("tiles"), lax.axis_index("diag")
    tiles, diags = lax.axis_size("tiles"), lax.axis_size("diag")
    par = [counts[0] * (ROWS // 4)] + [reach[n] for n in range(4)] + [dilation[0], dilation[1]]
    par += [tile, diag, tiles - 1, diags - 1]
    x_load = pltpu.make_async_copy(x_hbm, x_ref, load.at[0])
    g_load = pltpu.make_async_copy(g_hbm, g_ref, load.at[1])
    x_load.start()
    g_load.start()

    shares = (tiles // inner) * diags
    outer, other = lax.div(tile, inner), lax.rem(tile, inner)
    rank = outer * diags + diag
    friends = [lax.rem(rank + step, shares) for step in range(1, shares)]
    friend_ids = [(lax.div(to, diags) * inner + other, lax.rem(to, diags)) for to in friends]
    cousin_ids = [(outer * inner + lax.rem(other + step, inner), diag) for step in range(1, inner)]
    near = neighbours()
    barrier = pltpu.get_barrier_semaphore()
    for device in near + friend_ids + cousin_ids:
        pl.semaphore_signal(barrier, inc=1, device_id=device, device_id_type=MESH)

    keep = jnp.where(kept_cells(par), 1.0, 0.0).astype(BF)
    x_load.wait()
    turn_field(lambda c: jnp.maximum(x_ref[c], jnp.zeros((), BF)) * keep, held, field)
    pl.semaphore_wait(barrier, len(near) + len(friend_ids) + len(cousin_ids))
    halo1 = halo_copies(near, field, first1, last1, left1, right1, top1, bot1, send1, recv1)
    halo1[0].start()
    halo1[1].start()
    pack_edges(par, field, first1, last1)
    for copy in halo1[2:]:
        copy.start()
    place_weights(conv, mix, forward, backward)
    g_load.wait()
    turn_field(lambda c: g_ref[c] * keep, held, masked)
    for copy in halo1:
        copy.wait_recv()

    shift_rows(par, field, left1, right1, top1, bot1, moved)
    halo2 = halo_copies(near, grad_pre, first2, last2, left2, right2, top2, bot2, send2, recv2)
    ends = EDGE // STEP
    middle = COLS // STEP - 2 * ends
    conv_forward(par, (2 * ends, lambda at: at + (at // ends) * middle), moved, masked, forward, grad_pre, hidden)
    halo2[0].start()
    halo2[1].start()
    conv_forward(par, (middle, lambda at: at + ends), moved, masked, forward, grad_pre, hidden)
    pack_edges(par, grad_pre, first2, last2)
    for copy in halo2[2:]:
        copy.start()
    kernel_grads(par, moved, masked, grad_pre, hidden, acc)
    share_out(acc, part)
    sum1 = [remote(part.at[to], parts_in.at[rank], send3.at[n], recv3.at[n], friend_ids[n]) for n, to in enumerate(friends)]
    sum2 = [remote(far.at[other], far.at[other], send4.at[n], recv4.at[n], to) for n, to in enumerate(cousin_ids)]
    sum3 = [remote(done.at[rank], done.at[rank], send5.at[n], recv5.at[n], to) for n, to in enumerate(friend_ids)]
    for copy in sum1:
        copy.start()
    parts_in[rank] = part[rank]

    for copy in halo2:
        copy.wait_recv()
    shift_rows(par, grad_pre, left2, right2, top2, bot2, moved)
    for copy in sum1:
        copy.wait_recv()
    far[other] = jnp.sum(parts_in[...], axis=0)
    for copy in sum2:
        copy.start()
    blocks = COLS // STEP
    conv_back(par, 0, blocks // 2, moved, backward, spread)
    for copy in sum2:
        copy.wait_recv()
    done[rank] = jnp.sum(far[...], axis=0)
    for copy in sum3:
        copy.start()
    conv_back(par, blocks // 2, blocks // 2, moved, backward, spread)
    drain = finish(par, x_ref, g_ref, spread, out_hbm, leave)
    for copy in sum3:
        copy.wait_recv()
    per = PIECES // shares
    for n in range(PIECES):
        sum_ref[n] = done[n // per, n % per]
    for copy in halo1 + halo2 + sum1 + sum2 + sum3:
        copy.wait_send()
    drain()


def unpack_kernel(scale, held, total, out, conv_ref, mix_ref, stage, enter, leave):
    size = CH // MOVES
    at = [pl.ds(n * size, size) for n in range(MOVES)]
    enters = [pltpu.make_async_copy(held.at[at[n]], stage.at[at[n]], enter.at[n]) for n in range(MOVES)]
    leaves = [pltpu.make_async_copy(stage.at[at[n]], out.at[at[n]], leave.at[n]) for n in range(MOVES)]
    for copy in enters:
        copy.start()
    for g in range(CH // 8):
        row = jnp.concatenate([total[2 * g], total[2 * g + 1]], axis=1) * scale
        for s in range(TAPS):
            conv_ref[s, 8 * g:8 * g + 8, :] = row[:, s * CH:(s + 1) * CH]
        mix_ref[8 * g:8 * g + 8, :] = row[:, TAPS * CH:(TAPS + 1) * CH]
        if g == 0:
            for n in range(MOVES):
                enters[n].wait()
                leaves[n].start()
    for copy in leaves:
        copy.wait()


def specs(space, count):
    return [pl.BlockSpec(memory_space=space)] * count


def body(inputs, cotangent, conv_weight, mix_weight, counts, band_reach, dilation):
    shape = jax.ShapeDtypeStruct
    tiles, diags = lax.axis_size("tiles"), lax.axis_size("diag")
    inner = 16 if tiles == 64 else 2
    shares = (tiles // inner) * diags
    dma = lambda n: pltpu.SemaphoreType.DMA((n,))
    whole = pltpu.VMEM((CH, ROWS, COLS), BF)
    field = pltpu.VMEM((COLS, CH, ROWS), BF)
    pack = pltpu.VMEM((GROUPS, CH, ROWS), BF)
    side = pltpu.VMEM((EDGE, CH, ROWS), BF)
    ends = pltpu.VMEM((GROUPS + 2, CH, ROWS), BF)
    slots = lambda n: pltpu.VMEM((n, PIECES // shares, 8, 2 * ROWS), F32)
    halo = [pack, pack, side, side, ends, ends]
    grad_inputs, total = pl.pallas_call(
        functools.partial(everything, inner),
        out_shape=[shape((CH, ROWS, COLS), BF), shape((PIECES, 8, 2 * ROWS), F32)],
        in_specs=specs(pltpu.SMEM, 3) + specs(pl.ANY, 2) + specs(pltpu.VMEM, 2),
        out_specs=specs(pl.ANY, 1) + specs(pltpu.VMEM, 1),
        scratch_shapes=[
            whole, whole, field, field, field, field,
            pltpu.VMEM((3, COLS + 2 * EDGE, CH, ROWS), BF),
            pltpu.VMEM((COLS * TURN, ROWS), F32),
            pltpu.VMEM((CH * BACK, ROWS), F32),
            pltpu.VMEM(((TAPS + 1) * CH, ROWS), F32),
            pltpu.VMEM((2 * CH, KPAD), BF),
            pltpu.VMEM((CH, KPAD), BF),
            *halo, *halo,
            slots(shares), slots(shares), slots(inner), slots(shares),
            dma(2), dma(CH // 4), dma(8), dma(8), dma(8), dma(8),
            dma(shares - 1), dma(shares - 1), dma(inner - 1), dma(inner - 1), dma(shares - 1), dma(shares - 1),
        ],
        cost_estimate=pl.CostEstimate(flops=6 * CH * CH * TAPS * ROWS * COLS, bytes_accessed=3 * 2 * CH * ROWS * COLS,
                                      transcendentals=0),
        compiler_params=pltpu.CompilerParams(collective_id=0, has_side_effects=True, vmem_limit_bytes=VMEM_LIMIT),
    )(counts, band_reach, dilation, inputs, cotangent, conv_weight, mix_weight)
    cells = TPD * tiles * (ROWS // 4) * COLS * diags
    return pl.pallas_call(
        functools.partial(unpack_kernel, 1.0 / math.sqrt(cells)),
        out_shape=[shape((CH, ROWS, COLS), BF), shape((TAPS, CH, CH), F32), shape((CH, CH), F32)],
        in_specs=specs(pltpu.HBM, 1) + specs(pltpu.VMEM, 1),
        out_specs=specs(pltpu.HBM, 1) + specs(pltpu.VMEM, 2),
        scratch_shapes=[whole, dma(MOVES), dma(MOVES)],
        compiler_params=pltpu.CompilerParams(vmem_limit_bytes=VMEM_LIMIT),
    )(grad_inputs, total)


def solution(mesh):
    in_specs = (
        P(None, "tiles", "diag"),
        P(None, "tiles", "diag"),
        P(),
        P(),
        P("tiles"),
        P("tiles"),
        P(),
    )
    out_specs = (P(None, "tiles", "diag"), P(), P())
    return jax.shard_map(body, mesh=mesh, in_specs=in_specs, out_specs=out_specs, check_vma=False)
```

time: 97.5 us -> 52.6 us (0.54)
  Pallas kernels: 89.9 us -> 51.2 us
  local copies, waits for them, and re-layouts: 5.97 us -> 0 us
    pallas_call x6 -> x2, Pallas kernels: 89.9 us -> 51.2 us  [the longest x1 47.3 us: body(): pl.pallas_call(functools.partial(everything, inner), out_shape=[shape((CH...]
    unnamed x7 -> x0, local copies, waits for them, and re-layouts: 3.08 us -> none
    concatenate x1 -> x0, local copies, waits for them, and re-layouts: 1.3 us -> none  [body(): jnp.concatenate([counts * (ROWS // 4), band_reach, dilation, jnp.stack([j...]
    pad x2 -> x0, local copies, waits for them, and re-layouts: 1.28 us -> none  [the longest x1 0.65 us: body(): jnp.pad(forward_weight, ((0, 0), (0, KPAD - (TAPS + 1) * CH)))]
where the time goes in v3:
time: 52.6 us; the launch traced here: 52.4 us
  Pallas kernels  51.2 us (97%)
  between operations  1.29 us (2%)
    pallas_call x1, Pallas kernels, body(): pl.pallas_call(functools.partial(everything, inner), out_shape=[shape((CH...  47.3 us
    pallas_call x1, Pallas kernels, body(): pl.pallas_call(functools.partial(unpack_kernel, 1.0 / math.sqrt(cells)),...  3.89 us

profile of v3, /device:TPU:1, one launch (start us, length us, event | category | flops | bytes accessed | tf_op | source)
XLA Modules:
  0.0 52.4 jit_solution(15866491044284208884)
XLA Ops:
  1.3 47.3 %shard_map.94 = (bf16[48,128,128]{2,1,0:T(8,128)(2,1)}, f32[16,8,256]{2,1,0:T(8,128)}) custom-call(s32[1]{0:T(128)S(6)} %copy.10.counts, s32[4]{0:T(128)} %reach.1, s32[2]{0:T(128)} %dilation.1, bf16[48,128,128]{2,1,0:T(8,128)(2,1)} %x_hbm.1, bf16[48,128,128]{2,1,0:T(8,128)(2,1)} %g_hbm.1, bf16[9,48,48]{2,1,0:T(8,128)(2,1)} %conv.1, bf16[48,48]{1,0:T(8,128)(2,1)} %mix.1), custom_call_target="tpu_custom_call" | custom-call | flops 2038431744 | bytes 4718592 | tf_op jit(solution)/shard_map/pallas_call | solution.py:412
  48.6 3.9 %shard_map.95 = (bf16[48,128,128]{2,1,0:T(8,128)(2,1)}, f32[9,48,48]{2,1,0:T(8,128)}, f32[48,48]{1,0:T(8,128)}) custom-call(bf16[48,128,128]{2,1,0:T(8,128)(2,1)} %get-tuple-element.5.held, f32[16,8,256]{2,1,0:T(8,128)} %get-tuple-element.6.total), custom_call_target="tpu_custom_call" | custom-call | tf_op jit(solution)/shard_map/pallas_call | solution.py:435

commit v4 on v3

v4 whole, which is shorter than its diff:
```python
import functools
import math

import jax
import jax.numpy as jnp
from jax import lax
from jax.experimental import pallas as pl
from jax.experimental.pallas import tpu as pltpu
from jax.sharding import PartitionSpec as P

MESH = pl.DeviceIdType.MESH
TPD = 2
DMAX = 8
CH = 48
ROWS = 128
COLS = 128
EDGE = 2 * DMAX
GROUPS = COLS // EDGE
STEP = 8
TAPS = 9
KPAD = 512
VMEM_LIMIT = 56 * 1024 * 1024
BF = jnp.bfloat16
F32 = jnp.float32
LIVE, REACH, DIL, TILE, DIAG, LAST_TILE, LAST_DIAG = 0, 1, 5, 7, 8, 9, 10
TURN = 56
BACK = 136
PIECES = 16
LOADS = 3
MOVES = 4


def iota(shape, dim):
    return lax.broadcasted_iota(jnp.int32, shape, dim)


def reach_of(par, ids):
    reach = jnp.where(ids < 64, jnp.where(ids < 32, par[REACH], par[REACH + 1]),
                      jnp.where(ids < 96, par[REACH + 2], par[REACH + 3]))
    return jnp.where(ids < par[LIVE], reach, 0)


def tap_moves(par):
    moves = []
    for a in range(3):
        for b in range(3):
            row = (a - 1) * par[DIL]
            moves.append((a, (b - 1) * par[DIL + 1] - row))
    return moves


def pack_edges(par, field, first, last):
    lane = iota((1, 2 * ROWS), 1)
    near = lane % DMAX
    want = jnp.where(lane < ROWS, near, par[LIVE] - DMAX + near)
    place = jnp.where(lane < ROWS, (lane // DMAX + EDGE // 2) % EDGE, (lane - ROWS) // DMAX)
    hit = jnp.where(iota((ROWS, 2 * ROWS), 0) == want, 1.0, 0.0)
    out = jnp.zeros((GROUPS * CH, 2 * ROWS), F32)
    for kk in range(0, EDGE, 2):
        weight = jnp.concatenate([jnp.where(place == kk + n, hit, 0.0).astype(BF) for n in range(2)], axis=0)
        lhs = jnp.concatenate(
            [jnp.concatenate([field[(g + 1) * EDGE + kk + n] for g in range(GROUPS)], axis=0) for n in range(2)], axis=1)
        out += jnp.dot(lhs, weight, preferred_element_type=F32)
    out = out.astype(BF)
    for g in range(GROUPS):
        first[g] = out[g * CH:(g + 1) * CH, :ROWS]
        last[g] = out[g * CH:(g + 1) * CH, ROWS:]


def set_edges(par, left, right, field):
    for e in range(EDGE):
        low, high = left[e], right[e]
        field[e] = jnp.where(par[DIAG] > 0, low, jnp.zeros_like(low))
        field[EDGE + COLS + e] = jnp.where(par[DIAG] < par[LAST_DIAG], high, jnp.zeros_like(high))


def shift_rows(par, groups, field, top, bot, moved):
    half = ROWS // 2
    lane = iota((1, 2 * ROWS), 1)
    move = jnp.where(lane < ROWS, -par[DIL], par[DIL])
    want = (lane % ROWS) + move
    rows = iota((ROWS, 2 * ROWS), 0)
    inner = jnp.where(rows == want, 1.0, 0.0).astype(BF)
    has_top = par[TILE] > 0
    has_bot = par[TILE] < par[LAST_TILE]
    top_want = jnp.where((want < 0) & has_top, want + DMAX, -1)
    low = want - par[LIVE]
    bot_want = jnp.where((low >= 0) & (low < DMAX) & has_bot, low, -1)
    wants = [jnp.where(rows < half, top_want, bot_want), jnp.where(rows < half, bot_want, top_want)]
    outers = [jnp.where(rows % DMAX == w, 1.0, 0.0) for w in wants]
    place = (rows % half) // DMAX
    has_left = par[DIAG] > 0
    has_right = par[DIAG] < par[LAST_DIAG]
    tops = jnp.concatenate([top[g] for g in groups], axis=0)
    bots = jnp.concatenate([bot[g] for g in groups], axis=0)
    upper = iota(tops.shape, 1) < half
    halos = [jnp.where(upper, tops, bots), jnp.where(upper, bots, tops)]

    for part in range(2):
        def column(at, carry):
            kk = at + part * (EDGE // 2)
            weight = jnp.concatenate([inner, jnp.where(place == at, outers[part], 0.0).astype(BF)], axis=0)
            tiles = [field[g * EDGE + kk] for g in groups]
            lhs = jnp.concatenate([jnp.concatenate(tiles, axis=0), halos[part]], axis=1)
            out = jnp.dot(lhs, weight, preferred_element_type=F32)
            for n, g in enumerate(groups):
                piece = out[n * CH:(n + 1) * CH]
                if g == 0:
                    piece = jnp.where(has_left, piece, 0.0)
                if g == GROUPS + 1:
                    piece = jnp.where(has_right, piece, 0.0)
                piece = piece.astype(BF)
                moved[0, g * EDGE + kk] = piece[:, :ROWS]
                moved[1, g * EDGE + kk] = piece[:, ROWS:]
            return carry

        lax.fori_loop(0, EDGE // 2, column, 0, unroll=4)


def tapped(field, moved, a, k):
    return field[EDGE + k] if a == 1 else moved[a // 2, EDGE + k]


def pair(refs):
    return jnp.concatenate(refs, axis=1)


def eye():
    return jnp.where(iota((ROWS, ROWS), 0) == iota((ROWS, ROWS), 1), 1.0, 0.0).astype(BF)


def turn(one, value):
    return lax.dot_general(one, value, (((1,), (1,)), ((), ())), preferred_element_type=F32)


def turn_field(loads, value, held, put):
    one = eye()
    size = CH // len(loads)

    def channels(step, carry):
        c = step * 4
        out = turn(one, jnp.concatenate([value(c + n) for n in range(4)], axis=0))
        for n in range(4):
            held[pl.ds(c + n, COLS, stride=TURN), :] = out[:, n * ROWS:(n + 1) * ROWS]
        return carry

    for n, load in enumerate(loads):
        load.wait()
        lax.fori_loop(n * size // 4, (n + 1) * size // 4, channels, 0, unroll=size // 4)

    def column(k, carry):
        put(k, held[pl.ds(pl.multiple_of(k * TURN, 8), CH), :].astype(BF))
        return carry

    lax.fori_loop(0, COLS, column, 0, unroll=16)


def kept_cells(par):
    shape = (ROWS, COLS)
    return iota(shape, 1) + par[DIAG] * COLS < reach_of(par, iota(shape, 0))


def conv_forward(par, blocks, field, moved, masked, weight, grad_pre, hidden):
    moves = tap_moves(par)
    used = (TAPS + 1) * CH
    pad = jnp.zeros((KPAD - used, 2 * ROWS), BF)
    count, number = blocks

    def block(at, carry):
        for j in range(0, STEP, 2):
            k = number(at) * STEP + j
            tiles = [pair([tapped(field, moved, a, k + n + shift) for n in range(2)]) for a, shift in moves]
            tiles += [pair([masked[k], masked[k + 1]]), pad]
            out = jnp.dot(weight[...], jnp.concatenate(tiles, axis=0), preferred_element_type=F32)
            pre, back = out[:CH], out[CH:]
            grad = jnp.where(pre > 0, back, 0.0).astype(BF)
            act = jnp.maximum(pre, 0.0).astype(BF)
            for n in range(2):
                grad_pre[EDGE + k + n] = grad[:, n * ROWS:(n + 1) * ROWS]
                hidden[k + n] = act[:, n * ROWS:(n + 1) * ROWS]
        return carry

    lax.fori_loop(0, count, block, 0, unroll=4)


def kernel_grads(par, field, moved, masked, grad_pre, hidden, acc):
    moves = tap_moves(par)
    acc[...] = jnp.zeros_like(acc)

    def block(blk, carry):
        ks = [blk * STEP + j for j in range(STEP)]
        tiles = [pair([tapped(field, moved, a, k + shift) for k in ks]) for a, shift in moves]
        lhs = jnp.concatenate(tiles + [pair([hidden[k] for k in ks])], axis=0)
        rhs = jnp.concatenate([pair([grad_pre[EDGE + k] for k in ks]), pair([masked[k] for k in ks])], axis=0)
        acc[:, :2 * CH] += lax.dot_general(lhs, rhs, (((1,), (1,)), ((), ())), preferred_element_type=F32)
        return carry

    lax.fori_loop(0, COLS // STEP, block, 0, unroll=2)


def share_out(acc, part):
    flat = acc[...].T
    both = jnp.where(iota((CH, (TAPS + 1) * CH), 1) < TAPS * CH, flat[:CH], flat[CH:2 * CH])
    both = jnp.concatenate([both, jnp.zeros((CH, KPAD - (TAPS + 1) * CH), F32)], axis=1)
    per = part.shape[1]
    for n in range(PIECES):
        at, half = (n // 2) * 8, (n % 2) * 2 * ROWS
        piece = both[at:at + 8, half:half + 2 * ROWS] if at < CH else jnp.zeros((8, 2 * ROWS), F32)
        part[n // per, n % per] = piece


def place_weights(conv, mix, forward, backward):
    shape = (CH, KPAD)
    gap = iota(shape, 1) - iota(shape, 0)
    taps = jnp.zeros(shape, F32)
    back = jnp.zeros(shape, F32)
    for s in range(TAPS):
        put = jnp.where(gap == s * CH, 1.0, 0.0).astype(BF)
        taps += jnp.dot(conv[s], put, preferred_element_type=F32)
        back += lax.dot_general(conv[s], put, (((0,), (0,)), ((), ())), preferred_element_type=F32)
    put = jnp.where(gap == TAPS * CH, 1.0, 0.0).astype(BF)
    mixed = lax.dot_general(mix[...], put, (((0,), (0,)), ((), ())), preferred_element_type=F32)
    forward[...] = jnp.concatenate([taps, mixed], axis=0).astype(BF)
    backward[...] = back.astype(BF)


def conv_back(par, first, count, field, moved, weight, spread):
    moves = tap_moves(par)
    pad = jnp.zeros((KPAD - TAPS * CH, 2 * ROWS), BF)

    def block(blk, carry):
        for j in range(0, STEP, 2):
            k = blk * STEP + j
            tiles = [pair([tapped(field, moved, 2 - a, k + n - shift) for n in range(2)]) for a, shift in moves]
            out = jnp.dot(weight[...], jnp.concatenate(tiles + [pad], axis=0), preferred_element_type=F32)
            for n in range(2):
                spread[pl.ds(k + n, CH, stride=BACK), :] = out[:, n * ROWS:(n + 1) * ROWS]
        return carry

    lax.fori_loop(first, first + count, block, 0, unroll=4)


def finish(par, x_ref, g_ref, spread, out_ref):
    keep = jnp.where(kept_cells(par), 1.0, 0.0).astype(BF)
    live = jnp.where(iota((ROWS, COLS), 0) < par[LIVE], 1.0, 0.0).astype(BF)
    one = eye()
    zero = jnp.zeros((ROWS, COLS), BF)

    def channels(step, carry):
        c = step * 4
        parts = [spread[pl.ds(pl.multiple_of((c + n) * BACK, 8), COLS), :].astype(BF) for n in range(4)]
        out = turn(one, jnp.concatenate(parts, axis=0)).astype(BF)
        for n in range(4):
            part = jnp.where(x_ref[c + n] > zero, out[:, n * ROWS:(n + 1) * ROWS], zero)
            out_ref[c + n] = (g_ref[c + n] + part * keep) * live
        return carry

    lax.fori_loop(0, CH // 4, channels, 0, unroll=4)


def remote(src, dst, send, recv, device):
    return pltpu.make_async_remote_copy(src_ref=src, dst_ref=dst, send_sem=send, recv_sem=recv,
                                        device_id=device, device_id_type=MESH)


def neighbours():
    tile, diag = lax.axis_index("tiles"), lax.axis_index("diag")
    tiles, diags = lax.axis_size("tiles"), lax.axis_size("diag")
    up, down = lax.rem(tile + tiles - 1, tiles), lax.rem(tile + 1, tiles)
    lo, hi = lax.rem(diag + diags - 1, diags), lax.rem(diag + 1, diags)
    return [(tile, lo), (tile, hi), (up, diag), (down, diag), (up, lo), (up, hi), (down, lo), (down, hi)]


def halo_copies(near, field, first, last, left, right, top, bot, send, recv):
    inner = pl.ds(1, GROUPS)
    plan = [
        (field.at[pl.ds(EDGE, EDGE)], right),
        (field.at[pl.ds(COLS, EDGE)], left),
        (first, bot.at[inner]),
        (last, top.at[inner]),
        (first.at[0], bot.at[GROUPS + 1]),
        (first.at[GROUPS - 1], bot.at[0]),
        (last.at[0], top.at[GROUPS + 1]),
        (last.at[GROUPS - 1], top.at[0]),
    ]
    return [remote(src, dst, send.at[n], recv.at[n], near[n]) for n, (src, dst) in enumerate(plan)]


def unpack(scale, done, conv_ref, mix_ref):
    per = done.shape[1]
    for g in range(CH // 8):
        halves = [done[n // per, n % per] for n in (2 * g, 2 * g + 1)]
        row = jnp.concatenate(halves, axis=1) * scale
        for s in range(TAPS):
            conv_ref[s, 8 * g:8 * g + 8, :] = row[:, s * CH:(s + 1) * CH]
        mix_ref[8 * g:8 * g + 8, :] = row[:, TAPS * CH:(TAPS + 1) * CH]


def everything(inner, scale, counts, reach, dilation, x_hbm, g_hbm, conv, mix, out_ref, conv_ref, mix_ref,
               x_ref, g_ref, field, masked, grad_pre, hidden, moved, held, spread, acc, forward, backward,
               first1, last1, left1, right1, top1, bot1, first2, last2, left2, right2, top2, bot2,
               part, parts_in, far, done, load, send1, recv1, send2, recv2, send3, recv3, send4, recv4, send5, recv5):
    tile, diag = lax.axis_index("tiles"), lax.axis_index("diag")
    tiles, diags = lax.axis_size("tiles"), lax.axis_size("diag")
    par = [counts[0] * (ROWS // 4)] + [reach[n] for n in range(4)] + [dilation[0], dilation[1]]
    par += [tile, diag, tiles - 1, diags - 1]
    parts = [pl.ds(n * (CH // LOADS), CH // LOADS) for n in range(LOADS)]
    x_loads = [pltpu.make_async_copy(x_hbm.at[at], x_ref.at[at], load.at[n]) for n, at in enumerate(parts)]
    g_loads = [pltpu.make_async_copy(g_hbm.at[at], g_ref.at[at], load.at[LOADS + n]) for n, at in enumerate(parts)]
    for copy in x_loads + g_loads:
        copy.start()

    shares = (tiles // inner) * diags
    outer, other = lax.div(tile, inner), lax.rem(tile, inner)
    rank = outer * diags + diag
    friends = [lax.rem(rank + step, shares) for step in range(1, shares)]
    friend_ids = [(lax.div(to, diags) * inner + other, lax.rem(to, diags)) for to in friends]
    cousin_ids = [(outer * inner + lax.rem(other + step, inner), diag) for step in range(1, inner)]
    near = neighbours()
    barrier = pltpu.get_barrier_semaphore()
    for device in near + friend_ids + cousin_ids:
        pl.semaphore_signal(barrier, inc=1, device_id=device, device_id_type=MESH)

    keep = jnp.where(kept_cells(par), 1.0, 0.0).astype(BF)

    def put_field(k, value):
        field[EDGE + k] = value

    def put_masked(k, value):
        masked[k] = value

    turn_field(x_loads, lambda c: jnp.maximum(x_ref[c], jnp.zeros((), BF)) * keep, held, put_field)
    pl.semaphore_wait(barrier, len(near) + len(friend_ids) + len(cousin_ids))
    halo1 = halo_copies(near, field, first1, last1, left1, right1, top1, bot1, send1, recv1)
    halo1[0].start()
    halo1[1].start()
    pack_edges(par, field, first1, last1)
    for copy in halo1[2:]:
        copy.start()
    place_weights(conv, mix, forward, backward)
    turn_field(g_loads, lambda c: g_ref[c] * keep, held, put_masked)
    inside = range(1, GROUPS + 1)
    for copy in halo1[2:4]:
        copy.wait_recv()
    shift_rows(par, inside, field, top1, bot1, moved)
    halo2 = halo_copies(near, grad_pre, first2, last2, left2, right2, top2, bot2, send2, recv2)
    ends = EDGE // STEP
    middle = COLS // STEP - 2 * ends
    conv_forward(par, (middle, lambda at: at + ends), field, moved, masked, forward, grad_pre, hidden)
    for copy in halo1[:2] + halo1[4:]:
        copy.wait_recv()
    set_edges(par, left1, right1, field)
    shift_rows(par, [0, GROUPS + 1], field, top1, bot1, moved)
    conv_forward(par, (2 * ends, lambda at: at + (at // ends) * middle), field, moved, masked, forward, grad_pre, hidden)
    halo2[0].start()
    halo2[1].start()
    pack_edges(par, grad_pre, first2, last2)
    for copy in halo2[2:]:
        copy.start()
    kernel_grads(par, field, moved, masked, grad_pre, hidden, acc)
    share_out(acc, part)
    sum1 = [remote(part.at[to], parts_in.at[rank], send3, recv3, friend_ids[n]) for n, to in enumerate(friends)]
    sum2 = [remote(far.at[other], far.at[other], send4, recv4, to) for to in cousin_ids]
    sum3 = [remote(done.at[rank], done.at[rank], send5, recv5, to) for to in friend_ids]
    all1, all2, all3 = [
        remote(slots.at[pl.ds(0, slots.shape[0] - 1)], slots.at[pl.ds(0, slots.shape[0] - 1)], send, recv, near[0])
        for slots, send, recv in ((parts_in, send3, recv3), (far, send4, recv4), (done, send5, recv5))]
    for copy in sum1:
        copy.start()
    parts_in[rank] = part[rank]

    for copy in halo2:
        copy.wait_recv()
    set_edges(par, left2, right2, grad_pre)
    shift_rows(par, range(GROUPS + 2), grad_pre, top2, bot2, moved)
    all1.wait_recv()
    far[other] = jnp.sum(parts_in[...], axis=0)
    for copy in sum2:
        copy.start()
    blocks = COLS // STEP
    conv_back(par, 0, blocks // 2, grad_pre, moved, backward, spread)
    all2.wait_recv()
    done[rank] = jnp.sum(far[...], axis=0)
    for copy in sum3:
        copy.start()
    conv_back(par, blocks // 2, blocks // 2, grad_pre, moved, backward, spread)
    finish(par, x_ref, g_ref, spread, out_ref)
    all3.wait_recv()
    unpack(scale, done, conv_ref, mix_ref)
    for copy in halo1 + halo2 + [all1, all2, all3]:
        copy.wait_send()


def move_out(field, conv, mix, field_out, conv_out, mix_out, sems):
    size = CH // MOVES
    pieces = [(field.at[pl.ds(n * size, size)], field_out.at[pl.ds(n * size, size)]) for n in range(MOVES)]
    copies = [pltpu.make_async_copy(src, dst, sems.at[n])
              for n, (src, dst) in enumerate([(conv, conv_out), (mix, mix_out)] + pieces)]
    for copy in copies:
        copy.start()
    for copy in copies:
        copy.wait()


def specs(space, count):
    return [pl.BlockSpec(memory_space=space)] * count


def body(inputs, cotangent, conv_weight, mix_weight, counts, band_reach, dilation):
    shape = jax.ShapeDtypeStruct
    tiles, diags = lax.axis_size("tiles"), lax.axis_size("diag")
    inner = 16 if tiles == 64 else 2
    shares = (tiles // inner) * diags
    dma = lambda n: pltpu.SemaphoreType.DMA((n,))
    whole = pltpu.VMEM((CH, ROWS, COLS), BF)
    field = pltpu.VMEM((COLS, CH, ROWS), BF)
    pack = pltpu.VMEM((GROUPS, CH, ROWS), BF)
    wide = pltpu.VMEM((COLS + 2 * EDGE, CH, ROWS), BF)
    side = pltpu.VMEM((EDGE, CH, ROWS), BF)
    ends = pltpu.VMEM((GROUPS + 2, CH, ROWS), BF)
    slots = lambda n: pltpu.VMEM((n, PIECES // shares, 8, 2 * ROWS), F32)
    halo = [pack, pack, side, side, ends, ends]
    cells = TPD * tiles * (ROWS // 4) * COLS * diags
    results = pl.pallas_call(
        functools.partial(everything, inner, 1.0 / math.sqrt(cells)),
        out_shape=[pltpu.VMEM((CH, ROWS, COLS), BF), pltpu.VMEM((TAPS, CH, CH), F32), pltpu.VMEM((CH, CH), F32)],
        in_specs=specs(pltpu.SMEM, 3) + specs(pl.ANY, 2) + specs(pltpu.VMEM, 2),
        out_specs=specs(pltpu.VMEM, 3),
        scratch_shapes=[
            whole, whole, wide, field, wide, field,
            pltpu.VMEM((2, COLS + 2 * EDGE, CH, ROWS), BF),
            pltpu.VMEM(((COLS + 1) * TURN, ROWS), F32),
            pltpu.VMEM(((CH + 1) * BACK, ROWS), F32),
            pltpu.VMEM(((TAPS + 1) * CH, ROWS), F32),
            pltpu.VMEM((2 * CH, KPAD), BF),
            pltpu.VMEM((CH, KPAD), BF),
            *halo, *halo,
            slots(shares), slots(shares), slots(inner), slots(shares),
            dma(2 * LOADS), dma(8), dma(8), dma(8), dma(8),
            *[pltpu.SemaphoreType.DMA] * 6,
        ],
        cost_estimate=pl.CostEstimate(flops=6 * CH * CH * TAPS * ROWS * COLS, bytes_accessed=3 * 2 * CH * ROWS * COLS,
                                      transcendentals=0),
        compiler_params=pltpu.CompilerParams(collective_id=0, has_side_effects=True, vmem_limit_bytes=VMEM_LIMIT),
    )(counts, band_reach, dilation, inputs, cotangent, conv_weight, mix_weight)
    return pl.pallas_call(
        move_out,
        out_shape=[shape(r.shape, r.dtype) for r in results],
        in_specs=specs(pltpu.VMEM, 3),
        out_specs=specs(pltpu.HBM, 3),
        scratch_shapes=[dma(MOVES + 2)],
        compiler_params=pltpu.CompilerParams(vmem_limit_bytes=8 * 1024 * 1024),
    )(*results)


def solution(mesh):
    in_specs = (
        P(None, "tiles", "diag"),
        P(None, "tiles", "diag"),
        P(),
        P(),
        P("tiles"),
        P("tiles"),
        P(),
    )
    out_specs = (P(None, "tiles", "diag"), P(), P())
    return jax.shard_map(body, mesh=mesh, in_specs=in_specs, out_specs=out_specs, check_vma=False)
```

time: 52.6 us -> 46.3 us (0.88)
  Pallas kernels: 51.2 us -> 44.9 us
    pallas_call x2, Pallas kernels: 51.2 us -> 44.9 us  [the longest x1 43.6 us: body(): pl.pallas_call(functools.partial(everything, inner, 1.0 / math.sqrt(cells...]
where the time goes in v4:
time: 46.3 us; the launch traced here: 46.2 us
  Pallas kernels  44.9 us (97%)
  between operations  1.29 us (3%)
    pallas_call x1, Pallas kernels, body(): pl.pallas_call(functools.partial(everything, inner, 1.0 / math.sqrt(cells...  43.6 us
    pallas_call x1, Pallas kernels, body(): pl.pallas_call(move_out, out_shape=[shape(r.shape, r.dtype) for r in resu...  1.27 us

profile of v4, /device:TPU:1, one launch (start us, length us, event | category | flops | bytes accessed | tf_op | source)
XLA Modules:
  0.0 46.2 jit_solution(15280089821460978580)
XLA Ops:
  1.3 43.6 %shard_map.94 = (bf16[48,128,128]{2,1,0:T(8,128)(2,1)S(1)}, f32[9,48,48]{2,1,0:T(8,128)S(1)}, f32[48,48]{1,0:T(8,128)S(1)}) custom-call(s32[1]{0:T(128)S(6)} %copy.10.counts, s32[4]{0:T(128)} %reach.1, s32[2]{0:T(128)} %dilation.1, bf16[48,128,128]{2,1,0:T(8,128)(2,1)} %x_hbm.1, bf16[48,128,128]{2,1,0:T(8,128)(2,1)} %g_hbm.1, bf16[9,48,48]{2,1,0:T(8,128)(2,1)} %conv.1, ...), custom_call_target="tpu_custom_call" | custom-call | flops 2038431744 | bytes 4718592 | tf_op jit(solution)/shard_map/pallas_call | solution.py:424
  44.9 1.3 %shard_map.95 = (bf16[48,128,128]{2,1,0:T(8,128)(2,1)}, f32[9,48,48]{2,1,0:T(8,128)}, f32[48,48]{1,0:T(8,128)}) custom-call(bf16[48,128,128]{2,1,0:T(8,128)(2,1)S(1)} %get-tuple-element.6.field, f32[9,48,48]{2,1,0:T(8,128)S(1)} %get-tuple-element.7.conv, f32[48,48]{1,0:T(8,128)S(1)} %get-tuple-element.8.mix), custom_call_target="tpu_custom_call" | custom-call | tf_op jit(solution)/shard_map/pallas_call | solution.py:446

commit v5 on v4

--- a/solution.py
+++ b/solution.py
@@ -25,7 +25,6 @@
 LIVE, REACH, DIL, TILE, DIAG, LAST_TILE, LAST_DIAG = 0, 1, 5, 7, 8, 9, 10
 TURN = 56
 BACK = 136
-PIECES = 16
 LOADS = 3
 MOVES = 4
 
@@ -202,11 +201,10 @@
     flat = acc[...].T
     both = jnp.where(iota((CH, (TAPS + 1) * CH), 1) < TAPS * CH, flat[:CH], flat[CH:2 * CH])
     both = jnp.concatenate([both, jnp.zeros((CH, KPAD - (TAPS + 1) * CH), F32)], axis=1)
-    per = part.shape[1]
-    for n in range(PIECES):
-        at, half = (n // 2) * 8, (n % 2) * 2 * ROWS
-        piece = both[at:at + 8, half:half + 2 * ROWS] if at < CH else jnp.zeros((8, 2 * ROWS), F32)
-        part[n // per, n % per] = piece
+    rows = jnp.concatenate([both[:, n * ROWS:(n + 1) * ROWS] for n in range(KPAD // ROWS)], axis=0)
+    size = part.shape[1]
+    for n in range(part.shape[0]):
+        part[n] = rows[n * size:(n + 1) * size]
 
 
 def place_weights(conv, mix, forward, backward):
@@ -287,27 +285,26 @@
 
 
 def unpack(scale, done, conv_ref, mix_ref):
-    per = done.shape[1]
-    for g in range(CH // 8):
-        halves = [done[n // per, n % per] for n in (2 * g, 2 * g + 1)]
-        row = jnp.concatenate(halves, axis=1) * scale
-        for s in range(TAPS):
-            conv_ref[s, 8 * g:8 * g + 8, :] = row[:, s * CH:(s + 1) * CH]
-        mix_ref[8 * g:8 * g + 8, :] = row[:, TAPS * CH:(TAPS + 1) * CH]
-
-
-def everything(inner, scale, counts, reach, dilation, x_hbm, g_hbm, conv, mix, out_ref, conv_ref, mix_ref,
+    rows = jnp.concatenate([done[n] for n in range(done.shape[0])], axis=0) * scale
+    both = jnp.concatenate([rows[n * CH:(n + 1) * CH] for n in range(KPAD // ROWS)], axis=1)
+    for s in range(TAPS):
+        conv_ref[s] = both[:, s * CH:(s + 1) * CH]
+    mix_ref[...] = both[:, TAPS * CH:(TAPS + 1) * CH]
+
+
+def everything(inner, scale, counts_in, reach_in, dilation_in, x_hbm, g_hbm, conv_in, mix_in, out_ref, conv_ref, mix_ref,
+               counts, reach, dilation, conv, mix,
                x_ref, g_ref, field, masked, grad_pre, hidden, moved, held, spread, acc, forward, backward,
                first1, last1, left1, right1, top1, bot1, first2, last2, left2, right2, top2, bot2,
                part, parts_in, far, done, load, send1, recv1, send2, recv2, send3, recv3, send4, recv4, send5, recv5):
     tile, diag = lax.axis_index("tiles"), lax.axis_index("diag")
     tiles, diags = lax.axis_size("tiles"), lax.axis_size("diag")
-    par = [counts[0] * (ROWS // 4)] + [reach[n] for n in range(4)] + [dilation[0], dilation[1]]
-    par += [tile, diag, tiles - 1, diags - 1]
+    pairs = [(counts_in, counts), (reach_in, reach), (dilation_in, dilation), (conv_in, conv), (mix_in, mix)]
+    small = [pltpu.make_async_copy(src, dst, load.at[2 * LOADS + n]) for n, (src, dst) in enumerate(pairs)]
     parts = [pl.ds(n * (CH // LOADS), CH // LOADS) for n in range(LOADS)]
     x_loads = [pltpu.make_async_copy(x_hbm.at[at], x_ref.at[at], load.at[n]) for n, at in enumerate(parts)]
     g_loads = [pltpu.make_async_copy(g_hbm.at[at], g_ref.at[at], load.at[LOADS + n]) for n, at in enumerate(parts)]
-    for copy in x_loads + g_loads:
+    for copy in small + x_loads:
         copy.start()
 
     shares = (tiles // inner) * diags
@@ -321,6 +318,13 @@
     for device in near + friend_ids + cousin_ids:
         pl.semaphore_signal(barrier, inc=1, device_id=device, device_id_type=MESH)
 
+    for copy in g_loads:
+        copy.start()
+    for copy in small:
+        copy.wait()
+    par = [counts[0] * (ROWS // 4)] + [reach[n] for n in range(4)] + [dilation[0], dilation[1]]
+    par += [tile, diag, tiles - 1, diags - 1]
+    place_weights(conv, mix, forward, backward)
     keep = jnp.where(kept_cells(par), 1.0, 0.0).astype(BF)
 
     def put_field(k, value):
@@ -332,12 +336,9 @@
     turn_field(x_loads, lambda c: jnp.maximum(x_ref[c], jnp.zeros((), BF)) * keep, held, put_field)
     pl.semaphore_wait(barrier, len(near) + len(friend_ids) + len(cousin_ids))
     halo1 = halo_copies(near, field, first1, last1, left1, right1, top1, bot1, send1, recv1)
-    halo1[0].start()
-    halo1[1].start()
     pack_edges(par, field, first1, last1)
-    for copy in halo1[2:]:
-        copy.start()
-    place_weights(conv, mix, forward, backward)
+    for copy in halo1[2:] + halo1[:2]:
+        copy.start()
     turn_field(g_loads, lambda c: g_ref[c] * keep, held, put_masked)
     inside = range(1, GROUPS + 1)
     for copy in halo1[2:4]:
@@ -378,12 +379,13 @@
     for copy in sum2:
         copy.start()
     blocks = COLS // STEP
-    conv_back(par, 0, blocks // 2, grad_pre, moved, backward, spread)
+    early = blocks * 3 // 4
+    conv_back(par, 0, early, grad_pre, moved, backward, spread)
     all2.wait_recv()
     done[rank] = jnp.sum(far[...], axis=0)
     for copy in sum3:
         copy.start()
-    conv_back(par, blocks // 2, blocks // 2, grad_pre, moved, backward, spread)
+    conv_back(par, early, blocks - early, grad_pre, moved, backward, spread)
     finish(par, x_ref, g_ref, spread, out_ref)
     all3.wait_recv()
     unpack(scale, done, conv_ref, mix_ref)
@@ -418,15 +420,17 @@
     wide = pltpu.VMEM((COLS + 2 * EDGE, CH, ROWS), BF)
     side = pltpu.VMEM((EDGE, CH, ROWS), BF)
     ends = pltpu.VMEM((GROUPS + 2, CH, ROWS), BF)
-    slots = lambda n: pltpu.VMEM((n, PIECES // shares, 8, 2 * ROWS), F32)
+    slots = lambda n: pltpu.VMEM((n, CH * KPAD // ROWS // shares, ROWS), F32)
     halo = [pack, pack, side, side, ends, ends]
     cells = TPD * tiles * (ROWS // 4) * COLS * diags
     results = pl.pallas_call(
         functools.partial(everything, inner, 1.0 / math.sqrt(cells)),
         out_shape=[pltpu.VMEM((CH, ROWS, COLS), BF), pltpu.VMEM((TAPS, CH, CH), F32), pltpu.VMEM((CH, CH), F32)],
-        in_specs=specs(pltpu.SMEM, 3) + specs(pl.ANY, 2) + specs(pltpu.VMEM, 2),
+        in_specs=specs(pltpu.HBM, 7),
         out_specs=specs(pltpu.VMEM, 3),
         scratch_shapes=[
+            pltpu.SMEM(counts.shape, jnp.int32), pltpu.SMEM(band_reach.shape, jnp.int32), pltpu.SMEM(dilation.shape, jnp.int32),
+            pltpu.VMEM(conv_weight.shape, BF), pltpu.VMEM(mix_weight.shape, BF),
             whole, whole, wide, field, wide, field,
             pltpu.VMEM((2, COLS + 2 * EDGE, CH, ROWS), BF),
             pltpu.VMEM(((COLS + 1) * TURN, ROWS), F32),
@@ -436,7 +440,7 @@
             pltpu.VMEM((CH, KPAD), BF),
             *halo, *halo,
             slots(shares), slots(shares), slots(inner), slots(shares),
-            dma(2 * LOADS), dma(8), dma(8), dma(8), dma(8),
+            dma(2 * LOADS + 5), dma(8), dma(8), dma(8), dma(8),
             *[pltpu.SemaphoreType.DMA] * 6,
         ],
         cost_estimate=pl.CostEstimate(flops=6 * CH * CH * TAPS * ROWS * COLS, bytes_accessed=3 * 2 * CH * ROWS * COLS,

time: 46.3 us -> 44.6 us (0.963)
  Pallas kernels: 44.9 us -> 43.2 us
    pallas_call x1, Pallas kernels: 43.6 us -> 41.9 us  [body(): pl.pallas_call(functools.partial(everything, inner, 1.0 / math.sqrt(cells...]
where the time goes in v5:
time: 44.6 us; the launch traced here: 44.5 us
  Pallas kernels  43.2 us (97%)
  between operations  1.29 us (3%)
    pallas_call x1, Pallas kernels, body(): pl.pallas_call(functools.partial(everything, inner, 1.0 / math.sqrt(cells...  41.9 us
    pallas_call x1, Pallas kernels, body(): pl.pallas_call(move_out, out_shape=[shape(r.shape, r.dtype) for r in resu...  1.27 us

profile of v5, /device:TPU:1, one launch (start us, length us, event | category | flops | bytes accessed | tf_op | source)
XLA Modules:
  0.0 44.5 jit_solution(15678894405495123690)
XLA Ops:
  1.3 41.9 %shard_map.94 = (bf16[48,128,128]{2,1,0:T(8,128)(2,1)S(1)}, f32[9,48,48]{2,1,0:T(8,128)S(1)}, f32[48,48]{1,0:T(8,128)S(1)}) custom-call(s32[1]{0:T(128)S(6)} %copy.10.counts_in, s32[4]{0:T(128)} %reach_in.1, s32[2]{0:T(128)} %dilation_in.1, bf16[48,128,128]{2,1,0:T(8,128)(2,1)} %x_hbm.1, bf16[48,128,128]{2,1,0:T(8,128)(2,1)} %g_hbm.1, ...), custom_call_target="tpu_custom_call" | custom-call | flops 2038431744 | bytes 4718592 | tf_op jit(solution)/shard_map/pallas_call | solution.py:426
  43.2 1.3 %shard_map.95 = (bf16[48,128,128]{2,1,0:T(8,128)(2,1)}, f32[9,48,48]{2,1,0:T(8,128)}, f32[48,48]{1,0:T(8,128)}) custom-call(bf16[48,128,128]{2,1,0:T(8,128)(2,1)S(1)} %get-tuple-element.6.field, f32[9,48,48]{2,1,0:T(8,128)S(1)} %get-tuple-element.7.conv, f32[48,48]{1,0:T(8,128)S(1)} %get-tuple-element.8.mix), custom_call_target="tpu_custom_call" | custom-call | tf_op jit(solution)/shard_map/pallas_call | solution.py:450

commit v6 on v5

--- a/solution.py
+++ b/solution.py
@@ -54,13 +54,10 @@
     want = jnp.where(lane < ROWS, near, par[LIVE] - DMAX + near)
     place = jnp.where(lane < ROWS, (lane // DMAX + EDGE // 2) % EDGE, (lane - ROWS) // DMAX)
     hit = jnp.where(iota((ROWS, 2 * ROWS), 0) == want, 1.0, 0.0)
-    out = jnp.zeros((GROUPS * CH, 2 * ROWS), F32)
-    for kk in range(0, EDGE, 2):
-        weight = jnp.concatenate([jnp.where(place == kk + n, hit, 0.0).astype(BF) for n in range(2)], axis=0)
-        lhs = jnp.concatenate(
-            [jnp.concatenate([field[(g + 1) * EDGE + kk + n] for g in range(GROUPS)], axis=0) for n in range(2)], axis=1)
-        out += jnp.dot(lhs, weight, preferred_element_type=F32)
-    out = out.astype(BF)
+    weight = jnp.concatenate([jnp.where(place == kk, hit, 0.0).astype(BF) for kk in range(EDGE)], axis=0)
+    lhs = jnp.concatenate(
+        [jnp.concatenate([field[(g + 1) * EDGE + kk] for g in range(GROUPS)], axis=0) for kk in range(EDGE)], axis=1)
+    out = jnp.dot(lhs, weight, preferred_element_type=F32).astype(BF)
     for g in range(GROUPS):
         first[g] = out[g * CH:(g + 1) * CH, :ROWS]
         last[g] = out[g * CH:(g + 1) * CH, ROWS:]
@@ -185,22 +182,21 @@
 def kernel_grads(par, field, moved, masked, grad_pre, hidden, acc):
     moves = tap_moves(par)
     acc[...] = jnp.zeros_like(acc)
+    pad = jnp.zeros((KPAD - (TAPS + 1) * CH, STEP * ROWS), BF)
 
     def block(blk, carry):
         ks = [blk * STEP + j for j in range(STEP)]
         tiles = [pair([tapped(field, moved, a, k + shift) for k in ks]) for a, shift in moves]
-        lhs = jnp.concatenate(tiles + [pair([hidden[k] for k in ks])], axis=0)
-        rhs = jnp.concatenate([pair([grad_pre[EDGE + k] for k in ks]), pair([masked[k] for k in ks])], axis=0)
-        acc[:, :2 * CH] += lax.dot_general(lhs, rhs, (((1,), (1,)), ((), ())), preferred_element_type=F32)
+        rhs = jnp.concatenate(tiles + [pair([hidden[k] for k in ks]), pad], axis=0)
+        lhs = jnp.concatenate([pair([grad_pre[EDGE + k] for k in ks]), pair([masked[k] for k in ks])], axis=0)
+        acc[...] += lax.dot_general(lhs, rhs, (((1,), (1,)), ((), ())), preferred_element_type=F32)
         return carry
 
     lax.fori_loop(0, COLS // STEP, block, 0, unroll=2)
 
 
 def share_out(acc, part):
-    flat = acc[...].T
-    both = jnp.where(iota((CH, (TAPS + 1) * CH), 1) < TAPS * CH, flat[:CH], flat[CH:2 * CH])
-    both = jnp.concatenate([both, jnp.zeros((CH, KPAD - (TAPS + 1) * CH), F32)], axis=1)
+    both = jnp.where(iota((CH, KPAD), 1) < TAPS * CH, acc[:CH], acc[CH:])
     rows = jnp.concatenate([both[:, n * ROWS:(n + 1) * ROWS] for n in range(KPAD // ROWS)], axis=0)
     size = part.shape[1]
     for n in range(part.shape[0]):
@@ -435,7 +431,7 @@
             pltpu.VMEM((2, COLS + 2 * EDGE, CH, ROWS), BF),
             pltpu.VMEM(((COLS + 1) * TURN, ROWS), F32),
             pltpu.VMEM(((CH + 1) * BACK, ROWS), F32),
-            pltpu.VMEM(((TAPS + 1) * CH, ROWS), F32),
+            pltpu.VMEM((2 * CH, KPAD), F32),
             pltpu.VMEM((2 * CH, KPAD), BF),
             pltpu.VMEM((CH, KPAD), BF),
             *halo, *halo,

time: 44.6 us -> 44.9 us (level)
  no operation moved by 1% of the time
where the time goes in v6:
time: 44.9 us; the launch traced here: 44.8 us
  Pallas kernels  43.5 us (97%)
  between operations  1.29 us (3%)
    pallas_call x1, Pallas kernels, body(): pl.pallas_call(functools.partial(everything, inner, 1.0 / math.sqrt(cells...  42.2 us
    pallas_call x1, Pallas kernels, body(): pl.pallas_call(move_out, out_shape=[shape(r.shape, r.dtype) for r in resu...  1.27 us

profile of v6, /device:TPU:1, one launch (start us, length us, event | category | flops | bytes accessed | tf_op | source)
XLA Modules:
  0.0 44.8 jit_solution(13733043018857380722)
XLA Ops:
  1.3 42.2 %shard_map.94 = (bf16[48,128,128]{2,1,0:T(8,128)(2,1)S(1)}, f32[9,48,48]{2,1,0:T(8,128)S(1)}, f32[48,48]{1,0:T(8,128)S(1)}) custom-call(s32[1]{0:T(128)S(6)} %copy.10.counts_in, s32[4]{0:T(128)} %reach_in.1, s32[2]{0:T(128)} %dilation_in.1, bf16[48,128,128]{2,1,0:T(8,128)(2,1)} %x_hbm.1, bf16[48,128,128]{2,1,0:T(8,128)(2,1)} %g_hbm.1, ...), custom_call_target="tpu_custom_call" | custom-call | flops 2038431744 | bytes 4718592 | tf_op jit(solution)/shard_map/pallas_call | solution.py:422
  43.5 1.3 %shard_map.95 = (bf16[48,128,128]{2,1,0:T(8,128)(2,1)}, f32[9,48,48]{2,1,0:T(8,128)}, f32[48,48]{1,0:T(8,128)}) custom-call(bf16[48,128,128]{2,1,0:T(8,128)(2,1)S(1)} %get-tuple-element.6.field, f32[9,48,48]{2,1,0:T(8,128)S(1)} %get-tuple-element.7.conv, f32[48,48]{1,0:T(8,128)S(1)} %get-tuple-element.8.mix), custom_call_target="tpu_custom_call" | custom-call | tf_op jit(solution)/shard_map/pallas_call | solution.py:446

commit v7 on v6

--- a/solution.py
+++ b/solution.py
@@ -18,7 +18,7 @@
 GROUPS = COLS // EDGE
 STEP = 8
 TAPS = 9
-KPAD = 512
+SUM_ROWS = 192
 VMEM_LIMIT = 56 * 1024 * 1024
 BF = jnp.bfloat16
 F32 = jnp.float32
@@ -37,15 +37,6 @@
     reach = jnp.where(ids < 64, jnp.where(ids < 32, par[REACH], par[REACH + 1]),
                       jnp.where(ids < 96, par[REACH + 2], par[REACH + 3]))
     return jnp.where(ids < par[LIVE], reach, 0)
-
-
-def tap_moves(par):
-    moves = []
-    for a in range(3):
-        for b in range(3):
-            row = (a - 1) * par[DIL]
-            moves.append((a, (b - 1) * par[DIL + 1] - row))
-    return moves
 
 
 def pack_edges(par, field, first, last):
@@ -113,8 +104,9 @@
         lax.fori_loop(0, EDGE // 2, column, 0, unroll=4)
 
 
-def tapped(field, moved, a, k):
-    return field[EDGE + k] if a == 1 else moved[a // 2, EDGE + k]
+def stacked(par, field, moved, k):
+    step = par[DIL]
+    return jnp.concatenate([moved[0, EDGE + k + step], field[EDGE + k], moved[1, EDGE + k - step]], axis=0)
 
 
 def pair(refs):
@@ -156,82 +148,91 @@
     return iota(shape, 1) + par[DIAG] * COLS < reach_of(par, iota(shape, 0))
 
 
-def conv_forward(par, blocks, field, moved, masked, weight, grad_pre, hidden):
-    moves = tap_moves(par)
-    used = (TAPS + 1) * CH
-    pad = jnp.zeros((KPAD - used, 2 * ROWS), BF)
-    count, number = blocks
+def products(par, blocks, field, moved, weight, prod):
+    count, unroll, number = blocks
 
     def block(at, carry):
         for j in range(0, STEP, 2):
-            k = number(at) * STEP + j
-            tiles = [pair([tapped(field, moved, a, k + n + shift) for n in range(2)]) for a, shift in moves]
-            tiles += [pair([masked[k], masked[k + 1]]), pad]
-            out = jnp.dot(weight[...], jnp.concatenate(tiles, axis=0), preferred_element_type=F32)
-            pre, back = out[:CH], out[CH:]
-            grad = jnp.where(pre > 0, back, 0.0).astype(BF)
-            act = jnp.maximum(pre, 0.0).astype(BF)
+            k = number(at) + j
+            rhs = pair([stacked(par, field, moved, k), stacked(par, field, moved, k + 1)])
+            out = jnp.dot(weight[...], rhs, preferred_element_type=F32)
             for n in range(2):
-                grad_pre[EDGE + k + n] = grad[:, n * ROWS:(n + 1) * ROWS]
-                hidden[k + n] = act[:, n * ROWS:(n + 1) * ROWS]
-        return carry
-
-    lax.fori_loop(0, count, block, 0, unroll=4)
-
-
-def kernel_grads(par, field, moved, masked, grad_pre, hidden, acc):
-    moves = tap_moves(par)
+                prod[DMAX + k + n] = out[:, n * ROWS:(n + 1) * ROWS]
+        return carry
+
+    lax.fori_loop(0, count, block, 0, unroll=unroll)
+
+
+def gathered(par, prod, k):
+    step = par[DIL + 1]
+    return prod[DMAX + k - step, :CH] + prod[DMAX + k, CH:2 * CH] + prod[DMAX + k + step, 2 * CH:]
+
+
+def activate(par, blocks, prod, masked, mix_t, grad_pre, acc_mix):
+    count, number = blocks
+
+    def block(at, carry):
+        ks = [number(at) * STEP + j for j in range(STEP)]
+        upstream = pair([masked[k] for k in ks])
+        back = jnp.dot(mix_t[...], upstream, preferred_element_type=F32)
+        pre = pair([gathered(par, prod, k) for k in ks])
+        grad = jnp.where(pre > 0, back, 0.0).astype(BF)
+        for j, k in enumerate(ks):
+            grad_pre[EDGE + k] = grad[:, j * ROWS:(j + 1) * ROWS]
+        acc_mix[...] += lax.dot_general(upstream, jnp.maximum(pre, 0.0).astype(BF), (((1,), (1,)), ((), ())),
+                                        preferred_element_type=F32)
+        return carry
+
+    lax.fori_loop(0, count, block, 0, unroll=2)
+
+
+def kernel_grads(par, field, moved, grad_pre, acc):
     acc[...] = jnp.zeros_like(acc)
-    pad = jnp.zeros((KPAD - (TAPS + 1) * CH, STEP * ROWS), BF)
+    step = par[DIL + 1]
 
     def block(blk, carry):
-        ks = [blk * STEP + j for j in range(STEP)]
-        tiles = [pair([tapped(field, moved, a, k + shift) for k in ks]) for a, shift in moves]
-        rhs = jnp.concatenate(tiles + [pair([hidden[k] for k in ks]), pad], axis=0)
-        lhs = jnp.concatenate([pair([grad_pre[EDGE + k] for k in ks]), pair([masked[k] for k in ks])], axis=0)
+        ks = [blk * STEP - DMAX + j for j in range(STEP)]
+        rhs = pair([stacked(par, field, moved, k) for k in ks])
+        lhs = jnp.concatenate([pair([grad_pre[EDGE + k - move] for k in ks]) for move in (-step, 0, step)], axis=0)
         acc[...] += lax.dot_general(lhs, rhs, (((1,), (1,)), ((), ())), preferred_element_type=F32)
         return carry
 
-    lax.fori_loop(0, COLS // STEP, block, 0, unroll=2)
-
-
-def share_out(acc, part):
-    both = jnp.where(iota((CH, KPAD), 1) < TAPS * CH, acc[:CH], acc[CH:])
-    rows = jnp.concatenate([both[:, n * ROWS:(n + 1) * ROWS] for n in range(KPAD // ROWS)], axis=0)
+    lax.fori_loop(0, (COLS + 2 * DMAX) // STEP, block, 0, unroll=2)
+
+
+def share_out(acc, acc_mix, part):
+    main, side = acc[:, :ROWS], acc[:, ROWS:3 * CH]
+    tail = [side[n * CH:(n + 1) * CH] for n in range(3)] + [acc_mix[...], jnp.zeros((CH, 2 * EDGE), F32)]
+    rows = jnp.concatenate([main, jnp.concatenate(tail, axis=1)], axis=0)
     size = part.shape[1]
     for n in range(part.shape[0]):
         part[n] = rows[n * size:(n + 1) * size]
 
 
-def place_weights(conv, mix, forward, backward):
-    shape = (CH, KPAD)
+def place_weights(conv, mix, forward, backward, mix_t):
+    shape = (CH, 3 * CH)
     gap = iota(shape, 1) - iota(shape, 0)
-    taps = jnp.zeros(shape, F32)
-    back = jnp.zeros(shape, F32)
-    for s in range(TAPS):
-        put = jnp.where(gap == s * CH, 1.0, 0.0).astype(BF)
-        taps += jnp.dot(conv[s], put, preferred_element_type=F32)
-        back += lax.dot_general(conv[s], put, (((0,), (0,)), ((), ())), preferred_element_type=F32)
-    put = jnp.where(gap == TAPS * CH, 1.0, 0.0).astype(BF)
-    mixed = lax.dot_general(mix[...], put, (((0,), (0,)), ((), ())), preferred_element_type=F32)
-    forward[...] = jnp.concatenate([taps, mixed], axis=0).astype(BF)
-    backward[...] = back.astype(BF)
-
-
-def conv_back(par, first, count, field, moved, weight, spread):
-    moves = tap_moves(par)
-    pad = jnp.zeros((KPAD - TAPS * CH, 2 * ROWS), BF)
-
+    puts = [jnp.where(gap == a * CH, 1.0, 0.0).astype(BF) for a in range(3)]
+    turned = (((0,), (0,)), ((), ()))
+    for b in range(3):
+        taps = jnp.zeros(shape, F32)
+        back = jnp.zeros(shape, F32)
+        for a in range(3):
+            taps += jnp.dot(conv[3 * a + b], puts[a], preferred_element_type=F32)
+            back += lax.dot_general(conv[3 * (2 - a) + 2 - b], puts[a], turned, preferred_element_type=F32)
+        forward[b * CH:(b + 1) * CH, :] = taps.astype(BF)
+        backward[b * CH:(b + 1) * CH, :] = back.astype(BF)
+    mix_t[...] = lax.dot_general(mix[...], puts[0], turned, preferred_element_type=F32)[:, :CH].astype(BF)
+
+
+def lay_out(par, prod, spread):
     def block(blk, carry):
-        for j in range(0, STEP, 2):
+        for j in range(STEP):
             k = blk * STEP + j
-            tiles = [pair([tapped(field, moved, 2 - a, k + n - shift) for n in range(2)]) for a, shift in moves]
-            out = jnp.dot(weight[...], jnp.concatenate(tiles + [pad], axis=0), preferred_element_type=F32)
-            for n in range(2):
-                spread[pl.ds(k + n, CH, stride=BACK), :] = out[:, n * ROWS:(n + 1) * ROWS]
-        return carry
-
-    lax.fori_loop(first, first + count, block, 0, unroll=4)
+            spread[pl.ds(k, CH, stride=BACK), :] = gathered(par, prod, k)
+        return carry
+
+    lax.fori_loop(0, COLS // STEP, block, 0, unroll=2)
 
 
 def finish(par, x_ref, g_ref, spread, out_ref):
@@ -282,15 +283,17 @@
 
 def unpack(scale, done, conv_ref, mix_ref):
     rows = jnp.concatenate([done[n] for n in range(done.shape[0])], axis=0) * scale
-    both = jnp.concatenate([rows[n * CH:(n + 1) * CH] for n in range(KPAD // ROWS)], axis=1)
-    for s in range(TAPS):
-        conv_ref[s] = both[:, s * CH:(s + 1) * CH]
-    mix_ref[...] = both[:, TAPS * CH:(TAPS + 1) * CH]
+    tail = rows[3 * CH:]
+    for b in range(3):
+        full = jnp.concatenate([rows[b * CH:(b + 1) * CH], tail[:, b * EDGE:(b + 1) * EDGE]], axis=1)
+        for a in range(3):
+            conv_ref[3 * a + b] = full[:, a * CH:(a + 1) * CH]
+    mix_ref[...] = tail[:, 3 * EDGE:3 * EDGE + CH]
 
 
 def everything(inner, scale, counts_in, reach_in, dilation_in, x_hbm, g_hbm, conv_in, mix_in, out_ref, conv_ref, mix_ref,
                counts, reach, dilation, conv, mix,
-               x_ref, g_ref, field, masked, grad_pre, hidden, moved, held, spread, acc, forward, backward,
+               x_ref, g_ref, field, masked, grad_pre, prod, moved, held, spread, acc, acc_mix, forward, backward, mix_t,
                first1, last1, left1, right1, top1, bot1, first2, last2, left2, right2, top2, bot2,
                part, parts_in, far, done, load, send1, recv1, send2, recv2, send3, recv3, send4, recv4, send5, recv5):
     tile, diag = lax.axis_index("tiles"), lax.axis_index("diag")
@@ -320,7 +323,7 @@
         copy.wait()
     par = [counts[0] * (ROWS // 4)] + [reach[n] for n in range(4)] + [dilation[0], dilation[1]]
     par += [tile, diag, tiles - 1, diags - 1]
-    place_weights(conv, mix, forward, backward)
+    place_weights(conv, mix, forward, backward, mix_t)
     keep = jnp.where(kept_cells(par), 1.0, 0.0).astype(BF)
 
     def put_field(k, value):
@@ -343,19 +346,25 @@
     halo2 = halo_copies(near, grad_pre, first2, last2, left2, right2, top2, bot2, send2, recv2)
     ends = EDGE // STEP
     middle = COLS // STEP - 2 * ends
-    conv_forward(par, (middle, lambda at: at + ends), field, moved, masked, forward, grad_pre, hidden)
+    acc_mix[...] = jnp.zeros_like(acc_mix)
+    products(par, (middle + 2, 7, lambda at: at * STEP + DMAX), field, moved, forward, prod)
+    activate(par, (middle, lambda at: at + ends), prod, masked, mix_t, grad_pre, acc_mix)
     for copy in halo1[:2] + halo1[4:]:
         copy.wait_recv()
     set_edges(par, left1, right1, field)
     shift_rows(par, [0, GROUPS + 1], field, top1, bot1, moved)
-    conv_forward(par, (2 * ends, lambda at: at + (at // ends) * middle), field, moved, masked, forward, grad_pre, hidden)
+    products(par, (4, 4, lambda at: at * STEP - DMAX + (at // 2) * (middle + 2) * STEP), field, moved, forward, prod)
+    activate(par, (2 * ends, lambda at: at + (at // ends) * middle), prod, masked, mix_t, grad_pre, acc_mix)
     halo2[0].start()
     halo2[1].start()
     pack_edges(par, grad_pre, first2, last2)
     for copy in halo2[2:]:
         copy.start()
-    kernel_grads(par, field, moved, masked, grad_pre, hidden, acc)
-    share_out(acc, part)
+    for e in range(EDGE):
+        grad_pre[e] = jnp.zeros((CH, ROWS), BF)
+        grad_pre[EDGE + COLS + e] = jnp.zeros((CH, ROWS), BF)
+    kernel_grads(par, field, moved, grad_pre, acc)
+    share_out(acc, acc_mix, part)
     sum1 = [remote(part.at[to], parts_in.at[rank], send3, recv3, friend_ids[n]) for n, to in enumerate(friends)]
     sum2 = [remote(far.at[other], far.at[other], send4, recv4, to) for to in cousin_ids]
     sum3 = [remote(done.at[rank], done.at[rank], send5, recv5, to) for to in friend_ids]
@@ -374,14 +383,12 @@
     far[other] = jnp.sum(parts_in[...], axis=0)
     for copy in sum2:
         copy.start()
-    blocks = COLS // STEP
-    early = blocks * 3 // 4
-    conv_back(par, 0, early, grad_pre, moved, backward, spread)
+    products(par, (COLS // STEP + 2, 6, lambda at: at * STEP - DMAX), grad_pre, moved, backward, prod)
     all2.wait_recv()
     done[rank] = jnp.sum(far[...], axis=0)
     for copy in sum3:
         copy.start()
-    conv_back(par, early, blocks - early, grad_pre, moved, backward, spread)
+    lay_out(par, prod, spread)
     finish(par, x_ref, g_ref, spread, out_ref)
     all3.wait_recv()
     unpack(scale, done, conv_ref, mix_ref)
@@ -416,7 +423,7 @@
     wide = pltpu.VMEM((COLS + 2 * EDGE, CH, ROWS), BF)
     side = pltpu.VMEM((EDGE, CH, ROWS), BF)
     ends = pltpu.VMEM((GROUPS + 2, CH, ROWS), BF)
-    slots = lambda n: pltpu.VMEM((n, CH * KPAD // ROWS // shares, ROWS), F32)
+    slots = lambda n: pltpu.VMEM((n, SUM_ROWS // shares, ROWS), F32)
     halo = [pack, pack, side, side, ends, ends]
     cells = TPD * tiles * (ROWS // 4) * COLS * diags
     results = pl.pallas_call(
@@ -427,13 +434,16 @@
         scratch_shapes=[
             pltpu.SMEM(counts.shape, jnp.int32), pltpu.SMEM(band_reach.shape, jnp.int32), pltpu.SMEM(dilation.shape, jnp.int32),
             pltpu.VMEM(conv_weight.shape, BF), pltpu.VMEM(mix_weight.shape, BF),
-            whole, whole, wide, field, wide, field,
+            whole, whole, wide, field, wide,
+            pltpu.VMEM((COLS + 2 * DMAX, 3 * CH, ROWS), F32),
             pltpu.VMEM((2, COLS + 2 * EDGE, CH, ROWS), BF),
             pltpu.VMEM(((COLS + 1) * TURN, ROWS), F32),
             pltpu.VMEM(((CH + 1) * BACK, ROWS), F32),
-            pltpu.VMEM((2 * CH, KPAD), F32),
-            pltpu.VMEM((2 * CH, KPAD), BF),
-            pltpu.VMEM((CH, KPAD), BF),
+            pltpu.VMEM((3 * CH, 3 * CH), F32),
+            pltpu.VMEM((CH, CH), F32),
+            pltpu.VMEM((3 * CH, 3 * CH), BF),
+            pltpu.VMEM((3 * CH, 3 * CH), BF),
+            pltpu.VMEM((CH, CH), BF),
             *halo, *halo,
             slots(shares), slots(shares), slots(inner), slots(shares),
             dma(2 * LOADS + 5), dma(8), dma(8), dma(8), dma(8),

time: 44.9 us -> 43.9 us (0.978)
  Pallas kernels: 43.5 us -> 42.6 us
    pallas_call x1, Pallas kernels: 42.2 us -> 41.3 us  [body(): pl.pallas_call(functools.partial(everything, inner, 1.0 / math.sqrt(cells...]
where the time goes in v7:
time: 43.9 us; the launch traced here: 43.8 us
  Pallas kernels  42.6 us (97%)
  between operations  1.29 us (3%)
    pallas_call x1, Pallas kernels, body(): pl.pallas_call(functools.partial(everything, inner, 1.0 / math.sqrt(cells...  41.3 us
    pallas_call x1, Pallas kernels, body(): pl.pallas_call(move_out, out_shape=[shape(r.shape, r.dtype) for r in resu...  1.27 us

profile of v7, /device:TPU:1, one launch (start us, length us, event | category | flops | bytes accessed | tf_op | source)
XLA Modules:
  0.0 43.8 jit_solution(9203875139949262022)
XLA Ops:
  1.3 41.3 %shard_map.94 = (bf16[48,128,128]{2,1,0:T(8,128)(2,1)S(1)}, f32[9,48,48]{2,1,0:T(8,128)S(1)}, f32[48,48]{1,0:T(8,128)S(1)}) custom-call(s32[1]{0:T(128)S(6)} %copy.10.counts_in, s32[4]{0:T(128)} %reach_in.1, s32[2]{0:T(128)} %dilation_in.1, bf16[48,128,128]{2,1,0:T(8,128)(2,1)} %x_hbm.1, bf16[48,128,128]{2,1,0:T(8,128)(2,1)} %g_hbm.1, ...), custom_call_target="tpu_custom_call" | custom-call | flops 2038431744 | bytes 4718592 | tf_op jit(solution)/shard_map/pallas_call | solution.py:429
  42.6 1.3 %shard_map.95 = (bf16[48,128,128]{2,1,0:T(8,128)(2,1)}, f32[9,48,48]{2,1,0:T(8,128)}, f32[48,48]{1,0:T(8,128)}) custom-call(bf16[48,128,128]{2,1,0:T(8,128)(2,1)S(1)} %get-tuple-element.6.field, f32[9,48,48]{2,1,0:T(8,128)S(1)} %get-tuple-element.7.conv, f32[48,48]{1,0:T(8,128)S(1)} %get-tuple-element.8.mix), custom_call_target="tpu_custom_call" | custom-call | tf_op jit(solution)/shard_map/pallas_call | solution.py:456

commit v8 on v7

--- a/solution.py
+++ b/solution.py
@@ -291,11 +291,12 @@
     mix_ref[...] = tail[:, 3 * EDGE:3 * EDGE + CH]
 
 
-def everything(inner, scale, counts_in, reach_in, dilation_in, x_hbm, g_hbm, conv_in, mix_in, out_ref, conv_ref, mix_ref,
+def everything(depth, scale, counts_in, reach_in, dilation_in, x_hbm, g_hbm, conv_in, mix_in, out_ref, conv_ref, mix_ref,
                counts, reach, dilation, conv, mix,
                x_ref, g_ref, field, masked, grad_pre, prod, moved, held, spread, acc, acc_mix, forward, backward, mix_t,
                first1, last1, left1, right1, top1, bot1, first2, last2, left2, right2, top2, bot2,
-               part, parts_in, far, done, load, send1, recv1, send2, recv2, send3, recv3, send4, recv4, send5, recv5):
+               part, parts_in, over_diag, over_z, done, load, send1, recv1, send2, recv2,
+               send3, recv3, send4, recv4, send5, recv5, send6, recv6):
     tile, diag = lax.axis_index("tiles"), lax.axis_index("diag")
     tiles, diags = lax.axis_size("tiles"), lax.axis_size("diag")
     pairs = [(counts_in, counts), (reach_in, reach), (dilation_in, dilation), (conv_in, conv), (mix_in, mix)]
@@ -306,15 +307,16 @@
     for copy in small + x_loads:
         copy.start()
 
-    shares = (tiles // inner) * diags
-    outer, other = lax.div(tile, inner), lax.rem(tile, inner)
-    rank = outer * diags + diag
+    shares = (tiles // (2 * depth)) * 2
+    across, z, core = lax.div(tile, 2 * depth), lax.rem(lax.div(tile, 2), depth), lax.rem(tile, 2)
+    rank = across * 2 + core
     friends = [lax.rem(rank + step, shares) for step in range(1, shares)]
-    friend_ids = [(lax.div(to, diags) * inner + other, lax.rem(to, diags)) for to in friends]
-    cousin_ids = [(outer * inner + lax.rem(other + step, inner), diag) for step in range(1, inner)]
+    friend_ids = [(lax.div(to, 2) * 2 * depth + z * 2 + lax.rem(to, 2), diag) for to in friends]
+    diag_ids = [(tile, lax.rem(diag + step, diags)) for step in range(1, diags)]
+    z_ids = [((across * depth + lax.rem(z + step, depth)) * 2 + core, diag) for step in range(1, depth)]
     near = neighbours()
     barrier = pltpu.get_barrier_semaphore()
-    for device in near + friend_ids + cousin_ids:
+    for device in near + friend_ids + diag_ids + z_ids:
         pl.semaphore_signal(barrier, inc=1, device_id=device, device_id_type=MESH)
 
     for copy in g_loads:
@@ -333,7 +335,7 @@
         masked[k] = value
 
     turn_field(x_loads, lambda c: jnp.maximum(x_ref[c], jnp.zeros((), BF)) * keep, held, put_field)
-    pl.semaphore_wait(barrier, len(near) + len(friend_ids) + len(cousin_ids))
+    pl.semaphore_wait(barrier, len(near) + len(friend_ids) + len(diag_ids) + len(z_ids))
     halo1 = halo_copies(near, field, first1, last1, left1, right1, top1, bot1, send1, recv1)
     pack_edges(par, field, first1, last1)
     for copy in halo1[2:] + halo1[:2]:
@@ -366,11 +368,12 @@
     kernel_grads(par, field, moved, grad_pre, acc)
     share_out(acc, acc_mix, part)
     sum1 = [remote(part.at[to], parts_in.at[rank], send3, recv3, friend_ids[n]) for n, to in enumerate(friends)]
-    sum2 = [remote(far.at[other], far.at[other], send4, recv4, to) for to in cousin_ids]
-    sum3 = [remote(done.at[rank], done.at[rank], send5, recv5, to) for to in friend_ids]
-    all1, all2, all3 = [
+    sum2 = [remote(over_diag.at[diag], over_diag.at[diag], send4, recv4, to) for to in diag_ids]
+    sum3 = [remote(over_z.at[z], over_z.at[z], send5, recv5, to) for to in z_ids]
+    sum4 = [remote(done.at[rank], done.at[rank], send6, recv6, to) for to in friend_ids]
+    hops = [
         remote(slots.at[pl.ds(0, slots.shape[0] - 1)], slots.at[pl.ds(0, slots.shape[0] - 1)], send, recv, near[0])
-        for slots, send, recv in ((parts_in, send3, recv3), (far, send4, recv4), (done, send5, recv5))]
+        for slots, send, recv in ((parts_in, send3, recv3), (over_diag, send4, recv4), (over_z, send5, recv5), (done, send6, recv6))]
     for copy in sum1:
         copy.start()
     parts_in[rank] = part[rank]
@@ -379,20 +382,26 @@
         copy.wait_recv()
     set_edges(par, left2, right2, grad_pre)
     shift_rows(par, range(GROUPS + 2), grad_pre, top2, bot2, moved)
-    all1.wait_recv()
-    far[other] = jnp.sum(parts_in[...], axis=0)
+    hops[0].wait_recv()
+    over_diag[diag] = jnp.sum(parts_in[...], axis=0)
     for copy in sum2:
         copy.start()
-    products(par, (COLS // STEP + 2, 6, lambda at: at * STEP - DMAX), grad_pre, moved, backward, prod)
-    all2.wait_recv()
-    done[rank] = jnp.sum(far[...], axis=0)
+    half = (COLS // STEP + 2) // 2
+    products(par, (half, 3, lambda at: at * STEP - DMAX), grad_pre, moved, backward, prod)
+    hops[1].wait_recv()
+    over_z[z] = jnp.sum(over_diag[...], axis=0)
     for copy in sum3:
         copy.start()
+    products(par, (half, 3, lambda at: (at + half) * STEP - DMAX), grad_pre, moved, backward, prod)
     lay_out(par, prod, spread)
+    hops[2].wait_recv()
+    done[rank] = jnp.sum(over_z[...], axis=0)
+    for copy in sum4:
+        copy.start()
     finish(par, x_ref, g_ref, spread, out_ref)
-    all3.wait_recv()
+    hops[3].wait_recv()
     unpack(scale, done, conv_ref, mix_ref)
-    for copy in halo1 + halo2 + [all1, all2, all3]:
+    for copy in halo1 + halo2 + hops:
         copy.wait_send()
 
 
@@ -414,8 +423,8 @@
 def body(inputs, cotangent, conv_weight, mix_weight, counts, band_reach, dilation):
     shape = jax.ShapeDtypeStruct
     tiles, diags = lax.axis_size("tiles"), lax.axis_size("diag")
-    inner = 16 if tiles == 64 else 2
-    shares = (tiles // inner) * diags
+    depth = 8 if tiles == 64 else 2
+    shares = (tiles // (2 * depth)) * 2
     dma = lambda n: pltpu.SemaphoreType.DMA((n,))
     whole = pltpu.VMEM((CH, ROWS, COLS), BF)
     field = pltpu.VMEM((COLS, CH, ROWS), BF)
@@ -427,7 +436,7 @@
     halo = [pack, pack, side, side, ends, ends]
     cells = TPD * tiles * (ROWS // 4) * COLS * diags
     results = pl.pallas_call(
-        functools.partial(everything, inner, 1.0 / math.sqrt(cells)),
+        functools.partial(everything, depth, 1.0 / math.sqrt(cells)),
         out_shape=[pltpu.VMEM((CH, ROWS, COLS), BF), pltpu.VMEM((TAPS, CH, CH), F32), pltpu.VMEM((CH, CH), F32)],
         in_specs=specs(pltpu.HBM, 7),
         out_specs=specs(pltpu.VMEM, 3),
@@ -445,9 +454,9 @@
             pltpu.VMEM((3 * CH, 3 * CH), BF),
             pltpu.VMEM((CH, CH), BF),
             *halo, *halo,
-            slots(shares), slots(shares), slots(inner), slots(shares),
+            slots(shares), slots(shares), slots(diags), slots(depth), slots(shares),
             dma(2 * LOADS + 5), dma(8), dma(8), dma(8), dma(8),
-            *[pltpu.SemaphoreType.DMA] * 6,
+            *[pltpu.SemaphoreType.DMA] * 8,
         ],
         cost_estimate=pl.CostEstimate(flops=6 * CH * CH * TAPS * ROWS * COLS, bytes_accessed=3 * 2 * CH * ROWS * COLS,
                                       transcendentals=0),

time: 43.9 us -> 46.6 us (1.062)
  Pallas kernels: 42.6 us -> 45.2 us
    pallas_call x1, Pallas kernels: 41.3 us -> 43.9 us  [body(): pl.pallas_call(functools.partial(everything, depth, 1.0 / math.sqrt(cells...]
where the time goes in v8:
time: 46.6 us; the launch traced here: 46.5 us
  Pallas kernels  45.2 us (97%)
  between operations  1.29 us (3%)
    pallas_call x1, Pallas kernels, body(): pl.pallas_call(functools.partial(everything, depth, 1.0 / math.sqrt(cells...  43.9 us
    pallas_call x1, Pallas kernels, body(): pl.pallas_call(move_out, out_shape=[shape(r.shape, r.dtype) for r in resu...  1.27 us

profile of v8, /device:TPU:1, one launch (start us, length us, event | category | flops | bytes accessed | tf_op | source)
XLA Modules:
  0.0 46.5 jit_solution(3527911748599247416)
XLA Ops:
  1.3 43.9 %shard_map.94 = (bf16[48,128,128]{2,1,0:T(8,128)(2,1)S(1)}, f32[9,48,48]{2,1,0:T(8,128)S(1)}, f32[48,48]{1,0:T(8,128)S(1)}) custom-call(s32[1]{0:T(128)S(6)} %copy.10.counts_in, s32[4]{0:T(128)} %reach_in.1, s32[2]{0:T(128)} %dilation_in.1, bf16[48,128,128]{2,1,0:T(8,128)(2,1)} %x_hbm.1, bf16[48,128,128]{2,1,0:T(8,128)(2,1)} %g_hbm.1, ...), custom_call_target="tpu_custom_call" | custom-call | flops 2038431744 | bytes 4718592 | tf_op jit(solution)/shard_map/pallas_call | solution.py:438
  45.2 1.3 %shard_map.95 = (bf16[48,128,128]{2,1,0:T(8,128)(2,1)}, f32[9,48,48]{2,1,0:T(8,128)}, f32[48,48]{1,0:T(8,128)}) custom-call(bf16[48,128,128]{2,1,0:T(8,128)(2,1)S(1)} %get-tuple-element.6.field, f32[9,48,48]{2,1,0:T(8,128)S(1)} %get-tuple-element.7.conv, f32[48,48]{1,0:T(8,128)S(1)} %get-tuple-element.8.mix), custom_call_target="tpu_custom_call" | custom-call | tf_op jit(solution)/shard_map/pallas_call | solution.py:465

commit v9 on v7

--- a/solution.py
+++ b/solution.py
@@ -101,7 +101,7 @@
                 moved[1, g * EDGE + kk] = piece[:, ROWS:]
             return carry
 
-        lax.fori_loop(0, EDGE // 2, column, 0, unroll=4)
+        lax.fori_loop(0, EDGE // 2, column, 0, unroll=EDGE // 2)
 
 
 def stacked(par, field, moved, k):
@@ -183,7 +183,7 @@
                                         preferred_element_type=F32)
         return carry
 
-    lax.fori_loop(0, count, block, 0, unroll=2)
+    lax.fori_loop(0, count, block, 0, unroll=4)
 
 
 def kernel_grads(par, field, moved, grad_pre, acc):
@@ -197,7 +197,7 @@
         acc[...] += lax.dot_general(lhs, rhs, (((1,), (1,)), ((), ())), preferred_element_type=F32)
         return carry
 
-    lax.fori_loop(0, (COLS + 2 * DMAX) // STEP, block, 0, unroll=2)
+    lax.fori_loop(0, (COLS + 2 * DMAX) // STEP, block, 0, unroll=6)
 
 
 def share_out(acc, acc_mix, part):
@@ -266,6 +266,11 @@
     return [(tile, lo), (tile, hi), (up, diag), (down, diag), (up, lo), (up, hi), (down, lo), (down, hi)]
 
 
+def far_first(first, second):
+    moves = [(m, n) for m in range(first) for n in range(second) if m or n]
+    return sorted(moves, key=lambda move: -min(move[0], first - move[0]) - min(move[1], second - move[1]))
+
+
 def halo_copies(near, field, first, last, left, right, top, bot, send, recv):
     inner = pl.ds(1, GROUPS)
     plan = [
@@ -309,9 +314,12 @@
     shares = (tiles // inner) * diags
     outer, other = lax.div(tile, inner), lax.rem(tile, inner)
     rank = outer * diags + diag
-    friends = [lax.rem(rank + step, shares) for step in range(1, shares)]
-    friend_ids = [(lax.div(to, diags) * inner + other, lax.rem(to, diags)) for to in friends]
-    cousin_ids = [(outer * inner + lax.rem(other + step, inner), diag) for step in range(1, inner)]
+    friends = [(lax.rem(outer + dx, tiles // inner), lax.rem(diag + dy, diags)) for dx, dy in far_first(tiles // inner, diags)]
+    friend_ids = [(x * inner + other, y) for x, y in friends]
+    friends = [x * diags + y for x, y in friends]
+    deep, core = lax.div(other, 2), lax.rem(other, 2)
+    cousin_ids = [(outer * inner + lax.rem(deep + dz, inner // 2) * 2 + lax.rem(core + dc, 2), diag)
+                  for dz, dc in far_first(inner // 2, 2)]
     near = neighbours()
     barrier = pltpu.get_barrier_semaphore()
     for device in near + friend_ids + cousin_ids:
@@ -383,11 +391,13 @@
     far[other] = jnp.sum(parts_in[...], axis=0)
     for copy in sum2:
         copy.start()
-    products(par, (COLS // STEP + 2, 6, lambda at: at * STEP - DMAX), grad_pre, moved, backward, prod)
+    early = (COLS // STEP + 2) * 2 // 3
+    products(par, (early, 6, lambda at: at * STEP - DMAX), grad_pre, moved, backward, prod)
     all2.wait_recv()
     done[rank] = jnp.sum(far[...], axis=0)
     for copy in sum3:
         copy.start()
+    products(par, (early // 2, 6, lambda at: (at + early) * STEP - DMAX), grad_pre, moved, backward, prod)
     lay_out(par, prod, spread)
     finish(par, x_ref, g_ref, spread, out_ref)
     all3.wait_recv()

time: 43.9 us -> 41.7 us (0.950)
  Pallas kernels: 42.6 us -> 40.4 us
    pallas_call x1, Pallas kernels: 41.3 us -> 39.1 us  [body(): pl.pallas_call(functools.partial(everything, inner, 1.0 / math.sqrt(cells...]
where the time goes in v9:
time: 41.7 us
  Pallas kernels  40.4 us (97%)
  between operations  1.29 us (3%)
    pallas_call x1, Pallas kernels, body(): pl.pallas_call(functools.partial(everything, inner, 1.0 / math.sqrt(cells...  39.1 us
    pallas_call x1, Pallas kernels, body(): pl.pallas_call(move_out, out_shape=[shape(r.shape, r.dtype) for r in resu...  1.27 us

profile of v9, /device:TPU:1, one launch (start us, length us, event | category | flops | bytes accessed | tf_op | source)
XLA Modules:
  0.0 41.7 jit_solution(864670754550708283)
XLA Ops:
  1.3 39.1 %shard_map.94 = (bf16[48,128,128]{2,1,0:T(8,128)(2,1)S(1)}, f32[9,48,48]{2,1,0:T(8,128)S(1)}, f32[48,48]{1,0:T(8,128)S(1)}) custom-call(s32[1]{0:T(128)S(6)} %copy.10.counts_in, s32[4]{0:T(128)} %reach_in.1, s32[2]{0:T(128)} %dilation_in.1, bf16[48,128,128]{2,1,0:T(8,128)(2,1)} %x_hbm.1, bf16[48,128,128]{2,1,0:T(8,128)(2,1)} %g_hbm.1, ...), custom_call_target="tpu_custom_call" | custom-call | flops 2038431744 | bytes 4718592 | tf_op jit(solution)/shard_map/pallas_call | solution.py:439
  40.4 1.3 %shard_map.95 = (bf16[48,128,128]{2,1,0:T(8,128)(2,1)}, f32[9,48,48]{2,1,0:T(8,128)}, f32[48,48]{1,0:T(8,128)}) custom-call(bf16[48,128,128]{2,1,0:T(8,128)(2,1)S(1)} %get-tuple-element.6.field, f32[9,48,48]{2,1,0:T(8,128)S(1)} %get-tuple-element.7.conv, f32[48,48]{1,0:T(8,128)S(1)} %get-tuple-element.8.mix), custom_call_target="tpu_custom_call" | custom-call | tf_op jit(solution)/shard_map/pallas_call | solution.py:466

commit v10 on v9

--- a/solution.py
+++ b/solution.py
@@ -183,7 +183,7 @@
                                         preferred_element_type=F32)
         return carry
 
-    lax.fori_loop(0, count, block, 0, unroll=4)
+    lax.fori_loop(0, count, block, 0, unroll=min(count, 6))
 
 
 def kernel_grads(par, field, moved, grad_pre, acc):
@@ -197,7 +197,7 @@
         acc[...] += lax.dot_general(lhs, rhs, (((1,), (1,)), ((), ())), preferred_element_type=F32)
         return carry
 
-    lax.fori_loop(0, (COLS + 2 * DMAX) // STEP, block, 0, unroll=6)
+    lax.fori_loop(0, (COLS + 2 * DMAX) // STEP, block, 0, unroll=9)
 
 
 def share_out(acc, acc_mix, part):
@@ -232,7 +232,7 @@
             spread[pl.ds(k, CH, stride=BACK), :] = gathered(par, prod, k)
         return carry
 
-    lax.fori_loop(0, COLS // STEP, block, 0, unroll=2)
+    lax.fori_loop(0, COLS // STEP, block, 0, unroll=4)
 
 
 def finish(par, x_ref, g_ref, spread, out_ref):
@@ -250,7 +250,7 @@
             out_ref[c + n] = (g_ref[c + n] + part * keep) * live
         return carry
 
-    lax.fori_loop(0, CH // 4, channels, 0, unroll=4)
+    lax.fori_loop(0, CH // 4, channels, 0, unroll=6)
 
 
 def remote(src, dst, send, recv, device):
@@ -355,7 +355,7 @@
     ends = EDGE // STEP
     middle = COLS // STEP - 2 * ends
     acc_mix[...] = jnp.zeros_like(acc_mix)
-    products(par, (middle + 2, 7, lambda at: at * STEP + DMAX), field, moved, forward, prod)
+    products(par, (middle + 2, middle + 2, lambda at: at * STEP + DMAX), field, moved, forward, prod)
     activate(par, (middle, lambda at: at + ends), prod, masked, mix_t, grad_pre, acc_mix)
     for copy in halo1[:2] + halo1[4:]:
         copy.wait_recv()
@@ -392,7 +392,7 @@
     for copy in sum2:
         copy.start()
     early = (COLS // STEP + 2) * 2 // 3
-    products(par, (early, 6, lambda at: at * STEP - DMAX), grad_pre, moved, backward, prod)
+    products(par, (early, early, lambda at: at * STEP - DMAX), grad_pre, moved, backward, prod)
     all2.wait_recv()
     done[rank] = jnp.sum(far[...], axis=0)
     for copy in sum3:

time: 41.7 us -> 41.6 us (level)
  no operation moved by 1% of the time
where the time goes in v10:
time: 41.6 us; the launch traced here: 41.5 us
  Pallas kernels  40.2 us (97%)
  between operations  1.29 us (3%)
    pallas_call x1, Pallas kernels, body(): pl.pallas_call(functools.partial(everything, inner, 1.0 / math.sqrt(cells...  38.9 us
    pallas_call x1, Pallas kernels, body(): pl.pallas_call(move_out, out_shape=[shape(r.shape, r.dtype) for r in resu...  1.27 us

profile of v10, /device:TPU:1, one launch (start us, length us, event | category | flops | bytes accessed | tf_op | source)
XLA Modules:
  0.0 41.5 jit_solution(4387966195143614143)
XLA Ops:
  1.3 38.9 %shard_map.94 = (bf16[48,128,128]{2,1,0:T(8,128)(2,1)S(1)}, f32[9,48,48]{2,1,0:T(8,128)S(1)}, f32[48,48]{1,0:T(8,128)S(1)}) custom-call(s32[1]{0:T(128)S(6)} %copy.10.counts_in, s32[4]{0:T(128)} %reach_in.1, s32[2]{0:T(128)} %dilation_in.1, bf16[48,128,128]{2,1,0:T(8,128)(2,1)} %x_hbm.1, bf16[48,128,128]{2,1,0:T(8,128)(2,1)} %g_hbm.1, ...), custom_call_target="tpu_custom_call" | custom-call | flops 2038431744 | bytes 4718592 | tf_op jit(solution)/shard_map/pallas_call | solution.py:439
  40.2 1.3 %shard_map.95 = (bf16[48,128,128]{2,1,0:T(8,128)(2,1)}, f32[9,48,48]{2,1,0:T(8,128)}, f32[48,48]{1,0:T(8,128)}) custom-call(bf16[48,128,128]{2,1,0:T(8,128)(2,1)S(1)} %get-tuple-element.6.field, f32[9,48,48]{2,1,0:T(8,128)S(1)} %get-tuple-element.7.conv, f32[48,48]{1,0:T(8,128)S(1)} %get-tuple-element.8.mix), custom_call_target="tpu_custom_call" | custom-call | tf_op jit(solution)/shard_map/pallas_call | solution.py:466

commit v11 on v10

--- a/solution.py
+++ b/solution.py
@@ -183,7 +183,7 @@
                                         preferred_element_type=F32)
         return carry
 
-    lax.fori_loop(0, count, block, 0, unroll=min(count, 6))
+    lax.fori_loop(0, count, block, 0, unroll=count)
 
 
 def kernel_grads(par, field, moved, grad_pre, acc):
@@ -197,7 +197,7 @@
         acc[...] += lax.dot_general(lhs, rhs, (((1,), (1,)), ((), ())), preferred_element_type=F32)
         return carry
 
-    lax.fori_loop(0, (COLS + 2 * DMAX) // STEP, block, 0, unroll=9)
+    lax.fori_loop(0, (COLS + 2 * DMAX) // STEP, block, 0, unroll=18)
 
 
 def share_out(acc, acc_mix, part):
@@ -250,7 +250,7 @@
             out_ref[c + n] = (g_ref[c + n] + part * keep) * live
         return carry
 
-    lax.fori_loop(0, CH // 4, channels, 0, unroll=6)
+    lax.fori_loop(0, CH // 4, channels, 0, unroll=12)
 
 
 def remote(src, dst, send, recv, device):
@@ -391,13 +391,15 @@
     far[other] = jnp.sum(parts_in[...], axis=0)
     for copy in sum2:
         copy.start()
-    early = (COLS // STEP + 2) * 2 // 3
+    wide_blocks = COLS // STEP + 2
+    early = wide_blocks * 5 // 6
+    late = wide_blocks - early
     products(par, (early, early, lambda at: at * STEP - DMAX), grad_pre, moved, backward, prod)
     all2.wait_recv()
     done[rank] = jnp.sum(far[...], axis=0)
     for copy in sum3:
         copy.start()
-    products(par, (early // 2, 6, lambda at: (at + early) * STEP - DMAX), grad_pre, moved, backward, prod)
+    products(par, (late, late, lambda at: (at + early) * STEP - DMAX), grad_pre, moved, backward, prod)
     lay_out(par, prod, spread)
     finish(par, x_ref, g_ref, spread, out_ref)
     all3.wait_recv()

time: 41.6 us -> 41.5 us (level)
  no operation moved by 1% of the time
where the time goes in v11:
time: 41.5 us; the launch traced here: 41.4 us
  Pallas kernels  40.1 us (97%)
  between operations  1.29 us (3%)
    pallas_call x1, Pallas kernels, body(): pl.pallas_call(functools.partial(everything, inner, 1.0 / math.sqrt(cells...  38.8 us
    pallas_call x1, Pallas kernels, body(): pl.pallas_call(move_out, out_shape=[shape(r.shape, r.dtype) for r in resu...  1.27 us

profile of v11, /device:TPU:1, one launch (start us, length us, event | category | flops | bytes accessed | tf_op | source)
XLA Modules:
  0.0 41.4 jit_solution(9862438745673407082)
XLA Ops:
  1.3 38.8 %shard_map.94 = (bf16[48,128,128]{2,1,0:T(8,128)(2,1)S(1)}, f32[9,48,48]{2,1,0:T(8,128)S(1)}, f32[48,48]{1,0:T(8,128)S(1)}) custom-call(s32[1]{0:T(128)S(6)} %copy.10.counts_in, s32[4]{0:T(128)} %reach_in.1, s32[2]{0:T(128)} %dilation_in.1, bf16[48,128,128]{2,1,0:T(8,128)(2,1)} %x_hbm.1, bf16[48,128,128]{2,1,0:T(8,128)(2,1)} %g_hbm.1, ...), custom_call_target="tpu_custom_call" | custom-call | flops 2038431744 | bytes 4718592 | tf_op jit(solution)/shard_map/pallas_call | solution.py:441
  40.1 1.3 %shard_map.95 = (bf16[48,128,128]{2,1,0:T(8,128)(2,1)}, f32[9,48,48]{2,1,0:T(8,128)}, f32[48,48]{1,0:T(8,128)}) custom-call(bf16[48,128,128]{2,1,0:T(8,128)(2,1)S(1)} %get-tuple-element.6.field, f32[9,48,48]{2,1,0:T(8,128)S(1)} %get-tuple-element.7.conv, f32[48,48]{1,0:T(8,128)S(1)} %get-tuple-element.8.mix), custom_call_target="tpu_custom_call" | custom-call | tf_op jit(solution)/shard_map/pallas_call | solution.py:468
